TPU v7x, 1024 devices: a whole 4x8x16 slice. The times are simulated.
1024 devices in a mesh: patch: 128 (over z, x, core), elem: 8 (over y).
Axes of the slice: x: 4, y: 8, z: 16, core: 2. Of those that a mesh axis runs over, the one named last changes fastest.
Arguments:
- positions: float32 [3, 262144], P(None, ('patch', 'elem')), may hold values from -6 to 6
- target: float32 [3, 262144], P(None, ('patch', 'elem')), may hold values from -6 to 6
- inertia: float32 [1, 262144], P(None, ('patch', 'elem')), may hold values from 1 to 10
- incidence: int32 [3, 786432], P(None, ('patch', 'elem')), may hold values from 0 to 2047
- rest_inverse: float32 [4, 786432], P(None, ('patch', 'elem')), may hold values from -4 to 4
- counts: int32 [1024], P(('patch', 'elem')), may hold values from 192 to 768
- w_in: bfloat16 [128, 6], replicated, may hold values from -2.5 to 2.5
- w_hid1: bfloat16 [128, 128], replicated, may hold values from -0.5 to 0.5
- w_hid2: bfloat16 [128, 128], replicated, may hold values from -0.5 to 0.5
- w_out: bfloat16 [90, 128], replicated, may hold values from -0.5 to 0.5
Outputs:
- solution_field: float32 [3, 262144], P(None, ('patch', 'elem'))
- residual: float32 [3, 262144], P(None, ('patch', 'elem'))
All inputs are finite; a program needn't handle non-finite values.
Results may differ from a plain program's by a relative error of at most 0.0055.
Values sent between devices are 32-bit elements; how exact they have to be, the bound alone decides.
No kernel may reach another device: no remote copies, remote signals or barrier semaphores. Data moves between devices by JAX's collectives and lax.ppermute only.
A program may use at most 32 MiB of HBM per device.

v0:
```python
import jax
import jax.numpy as jnp
from jax import lax
from jax.sharding import PartitionSpec as P

ITERS = 3


STIFF = 1.0
REG = 0.1


def padded_2(shard, sides, width):
    for axis, dim in sides:
        size, length = (lax.axis_size(axis), shard.shape[dim])
        up = [(i, (i + 1) % size) for i in range(size - 1)]
        down = [(j, i) for i, j in up]
        last = lax.slice_in_dim(shard, length - width, length, axis=dim)
        first = lax.slice_in_dim(shard, 0, width, axis=dim)
        before = lax.ppermute(last, axis, up)
        after = lax.ppermute(first, axis, down)
        shard = jnp.concatenate([before, shard, after], axis=dim)
    return shard


def triangle_terms(pos, inc, rinv, valid, w_in, w_hid1, w_hid2, w_out):
    corner = [pos[:, inc[k]] for k in range(3)]
    edge_one = corner[1] - corner[0]
    edge_two = corner[2] - corner[0]
    feats = jnp.concatenate(
        [edge_one * rinv[0] + edge_two * rinv[2], edge_one * rinv[1] + edge_two * rinv[3]], axis=0
    ).astype(jnp.bfloat16)
    hidden = jnp.tanh(jnp.dot(w_in, feats, preferred_element_type=jnp.float32)).astype(jnp.bfloat16)
    hidden = jnp.tanh(jnp.dot(w_hid1, hidden, preferred_element_type=jnp.float32)).astype(
        jnp.bfloat16
    )
    hidden = jnp.tanh(jnp.dot(w_hid2, hidden, preferred_element_type=jnp.float32)).astype(
        jnp.bfloat16
    )
    output = jnp.dot(w_out, hidden, preferred_element_type=jnp.float32)
    stress = output[:9] * valid
    factor = (output[9:] * valid).astype(jnp.bfloat16)
    return (stress, factor)


def scatter_rows(values, inc, count):
    accum = jnp.zeros((3, count), jnp.float32)
    for k in range(3):
        accum = accum.at[:, inc[k]].add(values[3 * k : 3 * k + 3])
    return accum


def tri_apply(vec, inc, factor, valid, count):
    gathered = jnp.concatenate([vec[:, inc[k]] for k in range(3)], axis=0)
    full = factor.astype(jnp.float32).reshape(9, 9, -1)
    inner = jnp.sum(full * gathered[:, None, :], axis=0)
    result = jnp.sum(full * inner[None, :, :], axis=1) / 9.0 + REG * valid * gathered
    return scatter_rows(result, inc, count)


def chain_with(vec, rims):
    padded = rims(vec)
    return STIFF * (2.0 * vec - padded[:, :-2] - padded[:, 2:])


def per_device(
    positions, target, inertia, incidence, rest_inverse, counts, w_in, w_hid1, w_hid2, w_out
):
    vert_dev = positions.shape[1]
    groups = lax.axis_size("elem")
    patch_count = vert_dev * groups
    tri_slots = incidence.shape[1]
    valid = (jnp.arange(tri_slots, dtype=jnp.int32) < counts[0]).astype(jnp.float32)
    whole_pos = lax.all_gather(positions, "elem", axis=1, tiled=True)
    stress, factor = triangle_terms(
        whole_pos, incidence, rest_inverse, valid, w_in, w_hid1, w_hid2, w_out
    )
    full = factor.astype(jnp.float32).reshape(9, 9, tri_slots)
    hdiag = jnp.sum(full * full, axis=1) / 9.0 + REG * valid
    grad_local = scatter_rows(stress, incidence, patch_count)
    diag_local = scatter_rows(hdiag, incidence, patch_count)
    grad_tri, diag_tri = (
        lax.psum_scatter(grad_local, "elem", scatter_dimension=1, tiled=True),
        lax.psum_scatter(diag_local, "elem", scatter_dimension=1, tiled=True),
    )
    base_pos, base_target, base_inertia = (positions, target, inertia)

    def rims(vec):
        return padded_2(vec, ((("patch", "elem"), 1),), 1)

    def product(vec):
        whole = lax.all_gather(vec, "elem", axis=1, tiled=True)
        part = tri_apply(whole, incidence, factor, valid, patch_count)
        return lax.psum_scatter(part, "elem", scatter_dimension=1, tiled=True)

    def inner_pair(first, second):
        return lax.psum((first, second), ("patch", "elem"))

    def operate(vec):
        return base_inertia * vec + product(vec) + chain_with(vec, rims)

    gradient = base_inertia * (base_pos - base_target) + grad_tri + chain_with(base_pos, rims)
    diagonal = base_inertia + diag_tri + 2.0 * STIFF
    solution_field = jnp.zeros_like(base_pos)
    residual = -gradient
    precond = residual / diagonal
    image = operate(precond)
    gamma_now, delta = inner_pair(jnp.sum(residual * precond), jnp.sum(image * precond))
    alpha = gamma_now / delta
    direction, along = (precond, image)
    for step in range(ITERS):
        solution_field = solution_field + alpha * direction
        residual = residual - alpha * along
        if step + 1 < ITERS:
            precond = residual / diagonal
            image = operate(precond)
            gamma_next, delta = inner_pair(jnp.sum(residual * precond), jnp.sum(image * precond))
            ratio = gamma_next / gamma_now
            alpha = gamma_next / (delta - ratio * gamma_next / alpha)
            direction = precond + ratio * direction
            along = image + ratio * along
            gamma_now = gamma_next
    return (solution_field, residual)


def solution(mesh):
    placed = (
        P(None, ("patch", "elem")),
        P(None, ("patch", "elem")),
        P(None, ("patch", "elem")),
        P(None, ("patch", "elem")),
        P(None, ("patch", "elem")),
        P(("patch", "elem")),
        P(),
        P(),
        P(),
        P(),
    )
    return jax.shard_map(
        per_device,
        mesh=mesh,
        in_specs=placed,
        out_specs=(P(None, ("patch", "elem")), P(None, ("patch", "elem"))),
        check_vma=False,
    )
```

profile of v0, /device:TPU:1, one launch (start us, length us, event | category | flops | bytes accessed | tf_op | source)
XLA Modules:
  0.0 841.9 jit_solution(3490993322523143198)
XLA Ops:
  8.2 22.9 %all_gather.12 = f32[3,2048]{0,1:T(8,128)S(1)} all-gather(f32[3,256]{0,1:T(8,128)S(1)} %copy.147), channel_id=1, replica_groups=mesh['patch'=128,'elem'=8] {'elem'}, dimensions={1}, use_global_device_ids=true | all-gather | bytes 27648 | tf_op jit(solution)/shard_map/all_gather | solution.py:74
  46.4 6.4 scatter_fusion
  52.8 6.4 scatter_fusion.1
  67.6 6.4 scatter_fusion.2
  74.1 6.4 scatter_fusion.3
  84.8 18.1 %collective-permute-start.1 = (f32[3,1]{1,0:T(4,128)S(1)}, f32[3,1]{1,0:T(4,128)S(1)}, u32[]{:S(2)}, u32[]{:S(2)}) collective-permute-start(f32[3,1]{1,0:T(4,128)S(1)} %get-tuple-element.61), channel_id=1, source_target_pairs={{1,0},{2,1},{3,2},{4,3},{5,4},{6,5},{7,6},{8,7},{9,8},{10,9},{11,1... | collective-permute-start | bytes 44 | tf_op jit(solution)/shard_map/ppermute | solution.py:21
  102.9 11.8 %reduce-scatter.16.cloned.1.call-done = f32[256,3]{1,0:T(8,128)} async-done(((f32[2048,3]{1,0:T(8,128)}), f32[256,3]{1,0:T(8,128)}) %reduce-scatter.16.cloned.1.call-update) | async-done | bytes 3088
  115.7 48.1 %reduce-scatter.18.cloned.1.call-done = f32[256,3]{1,0:T(8,128)} async-done(((f32[2048,3]{1,0:T(8,128)}), f32[256,3]{1,0:T(8,128)}) %reduce-scatter.18.cloned.1.call-update) | async-done | bytes 3088
  165.5 18.3 %all_gather.13 = f32[3,2048]{1,0:T(4,128)S(1)} all-gather(f32[3,256]{1,0:T(4,128)S(1)} %get-tuple-element.33), channel_id=1, replica_groups=mesh['patch'=128,'elem'=8] {'elem'}, dimensions={1}, use_global_device_ids=true | all-gather | bytes 27648 | tf_op jit(solution)/shard_map/all_gather | solution.py:92
  196.5 6.4 scatter_fusion.4
  202.9 6.4 scatter_fusion.5
  213.1 15.4 %collective-permute-start.3 = (f32[3,1]{1,0:T(4,128)S(1)}, f32[3,1]{1,0:T(4,128)S(1)}, u32[]{:S(2)}, u32[]{:S(2)}) collective-permute-start(f32[3,1]{1,0:T(4,128)S(1)} %get-tuple-element.59), channel_id=1, source_target_pairs={{1,0},{2,1},{3,2},{4,3},{5,4},{6,5},{7,6},{8,7},{9,8},{10,9},{11,1... | collective-permute-start | bytes 44 | tf_op jit(solution)/shard_map/ppermute | solution.py:21
  228.5 34.1 %reduce-scatter.20.cloned.1.call-done = f32[256,3]{1,0:T(8,128)} async-done(((f32[2048,3]{1,0:T(8,128)}), f32[256,3]{1,0:T(8,128)}) %reduce-scatter.20.cloned.1.call-update) | async-done | bytes 3088
  264.3 127.8 %all-reduce.2 = (f32[]{:T(128)}, f32[]{:T(128)}) all-reduce(f32[]{:T(128)} %get-tuple-element.20, f32[]{:T(128)} %get-tuple-element.19), channel_id=1, replica_groups=mesh['patch'=128,'elem'=8] {'patch','elem'}, use_global_device_ids=true, to_apply=%region_10.0 | all-reduce | flops 2 | bytes 16 | tf_op jit(solution)/shard_map/psum | solution.py:97
  393.5 18.5 %all_gather.14 = f32[3,2048]{1,0:T(4,128)S(1)} all-gather(f32[3,256]{1,0:T(4,128)S(1)} %get-tuple-element.30), channel_id=1, replica_groups=mesh['patch'=128,'elem'=8] {'elem'}, dimensions={1}, use_global_device_ids=true | all-gather | bytes 27648 | tf_op jit(solution)/shard_map/all_gather | solution.py:92
  424.6 6.4 scatter_fusion.6
  440.6 8.6 %collective-permute-start.5 = (f32[3,1]{1,0:T(4,128)S(1)}, f32[3,1]{1,0:T(4,128)S(1)}, u32[]{:S(2)}, u32[]{:S(2)}) collective-permute-start(f32[3,1]{1,0:T(4,128)S(1)} %get-tuple-element.57), channel_id=1, source_target_pairs={{1,0},{2,1},{3,2},{4,3},{5,4},{6,5},{7,6},{8,7},{9,8},{10,9},{11,1... | collective-permute-start | bytes 44 | tf_op jit(solution)/shard_map/ppermute | solution.py:21
  449.1 31.1 %reduce-scatter.22.cloned.1.call-done = f32[256,3]{1,0:T(8,128)} async-done(((f32[2048,3]{1,0:T(8,128)}), f32[256,3]{1,0:T(8,128)}) %reduce-scatter.22.cloned.1.call-update) | async-done | bytes 3088
  482.0 127.9 %all-reduce.1 = (f32[]{:T(128)}, f32[]{:T(128)}) all-reduce(f32[]{:T(128)} %get-tuple-element.18, f32[]{:T(128)} %get-tuple-element.17), channel_id=1, replica_groups=mesh['patch'=128,'elem'=8] {'patch','elem'}, use_global_device_ids=true, to_apply=%region_20.0 | all-reduce | flops 2 | bytes 16 | tf_op jit(solution)/shard_map/psum | solution.py:97
  614.4 18.3 %all_gather.15 = f32[3,2048]{1,0:T(4,128)S(1)} all-gather(f32[3,256]{1,0:T(4,128)S(1)} %get-tuple-element.27), channel_id=1, replica_groups=mesh['patch'=128,'elem'=8] {'elem'}, dimensions={1}, use_global_device_ids=true | all-gather | bytes 27648 | tf_op jit(solution)/shard_map/all_gather | solution.py:92
  645.4 6.4 scatter_fusion.8
  661.3 8.6 %collective-permute-start.7 = (f32[3,1]{1,0:T(4,128)S(1)}, f32[3,1]{1,0:T(4,128)S(1)}, u32[]{:S(2)}, u32[]{:S(2)}) collective-permute-start(f32[3,1]{1,0:T(4,128)S(1)} %get-tuple-element.55), channel_id=1, source_target_pairs={{1,0},{2,1},{3,2},{4,3},{5,4},{6,5},{7,6},{8,7},{9,8},{10,9},{11,1... | collective-permute-start | bytes 44 | tf_op jit(solution)/shard_map/ppermute | solution.py:21
  669.8 31.2 %reduce-scatter.24.cloned.1.call-done = f32[256,3]{1,0:T(8,128)} async-done(((f32[2048,3]{1,0:T(8,128)}), f32[256,3]{1,0:T(8,128)}) %reduce-scatter.24.cloned.1.call-update) | async-done | bytes 3088
  702.7 127.9 %all-reduce = (f32[]{:T(128)}, f32[]{:T(128)}) all-reduce(f32[]{:T(128)} %get-tuple-element.16, f32[]{:T(128)} %get-tuple-element.15), channel_id=1, replica_groups=mesh['patch'=128,'elem'=8] {'patch','elem'}, use_global_device_ids=true, to_apply=%region_30.0 | all-reduce | flops 2 | bytes 16 | tf_op jit(solution)/shard_map/psum | solution.py:97
  (145 shorter events, 96.7 us)
Async XLA Ops:
  7.2 30.5 %copy-start = (bf16[128,128]{1,0:T(8,128)(2,1)S(1)}, bf16[128,128]{1,0:T(8,128)(2,1)}, u32[]{:S(2)}) copy-start(bf16[128,128]{1,0:T(8,128)(2,1)} %param.17) | copy-start | bytes 98308
  7.2 0.9 copy-start.7
  7.2 107.5 %reduce-scatter.16.cloned.1.call-start = ((), (), s32[]{:S(2)}) async-start(), calls=%async_computation.5 | async-start | bytes 1179648
  36.2 0.7 copy-start.10
  38.3 0.8 copy-start.8
  38.3 0.8 copy-start.9
  59.3 1.0 copy-start.5
  60.3 103.4 %reduce-scatter.18.cloned.1.call-start = ((), (), s32[]{:S(2)}) async-start(), calls=%async_computation.6 | async-start | bytes 1179648
  80.5 1.0 copy-start.2
  81.5 181.0 %reduce-scatter.20.cloned.1.call-start = ((), (), s32[]{:S(2)}) async-start(), calls=%async_computation.7 | async-start | bytes 1179648
  81.7 83.1 %collective-permute-start = (f32[3,1]{1,0:T(4,128)S(1)}, f32[3,1]{1,0:T(4,128)S(1)}, u32[]{:S(2)}, u32[]{:S(2)}) collective-permute-start(f32[3,1]{1,0:T(4,128)S(1)} %get-tuple-element.60), channel_id=1, source_target_pairs={{0,1},{1,2},{2,3},{3,4},{4,5},{5,6},{6,7},{7,8},{8,9},{9,10},{10,1... | collective-permute-start | bytes 44 | tf_op jit(solution)/shard_map/ppermute | solution.py:20
  84.8 80.0 %collective-permute-start.1 = (f32[3,1]{1,0:T(4,128)S(1)}, f32[3,1]{1,0:T(4,128)S(1)}, u32[]{:S(2)}, u32[]{:S(2)}) collective-permute-start(f32[3,1]{1,0:T(4,128)S(1)} %get-tuple-element.61), channel_id=1, source_target_pairs={{1,0},{2,1},{3,2},{4,3},{5,4},{6,5},{7,6},{8,7},{9,8},{10,9},{11,1... | collective-permute-start | bytes 44 | tf_op jit(solution)/shard_map/ppermute | solution.py:21
  163.8 1.0 copy-start.11
  209.4 1.0 copy-start.3
  210.4 269.8 %reduce-scatter.22.cloned.1.call-start = ((), (), s32[]{:S(2)}) async-start(), calls=%async_computation.8 | async-start | bytes 1179648
  210.5 53.0 %collective-permute-start.2 = (f32[3,1]{1,0:T(4,128)S(1)}, f32[3,1]{1,0:T(4,128)S(1)}, u32[]{:S(2)}, u32[]{:S(2)}) collective-permute-start(f32[3,1]{1,0:T(4,128)S(1)} %get-tuple-element.58), channel_id=1, source_target_pairs={{0,1},{1,2},{2,3},{3,4},{4,5},{5,6},{6,7},{7,8},{8,9},{9,10},{10,1... | collective-permute-start | bytes 44 | tf_op jit(solution)/shard_map/ppermute | solution.py:20
  213.1 50.5 %collective-permute-start.3 = (f32[3,1]{1,0:T(4,128)S(1)}, f32[3,1]{1,0:T(4,128)S(1)}, u32[]{:S(2)}, u32[]{:S(2)}) collective-permute-start(f32[3,1]{1,0:T(4,128)S(1)} %get-tuple-element.59), channel_id=1, source_target_pairs={{1,0},{2,1},{3,2},{4,3},{5,4},{6,5},{7,6},{8,7},{9,8},{10,9},{11,1... | collective-permute-start | bytes 44 | tf_op jit(solution)/shard_map/ppermute | solution.py:21
  437.5 1.0 copy-start.4
  438.5 262.5 %reduce-scatter.24.cloned.1.call-start = ((), (), s32[]{:S(2)}) async-start(), calls=%async_computation.9 | async-start | bytes 1179648
  438.7 42.5 %collective-permute-start.4 = (f32[3,1]{1,0:T(4,128)S(1)}, f32[3,1]{1,0:T(4,128)S(1)}, u32[]{:S(2)}, u32[]{:S(2)}) collective-permute-start(f32[3,1]{1,0:T(4,128)S(1)} %get-tuple-element.56), channel_id=1, source_target_pairs={{0,1},{1,2},{2,3},{3,4},{4,5},{5,6},{6,7},{7,8},{8,9},{9,10},{10,1... | collective-permute-start | bytes 44 | tf_op jit(solution)/shard_map/ppermute | solution.py:20
  440.6 40.6 %collective-permute-start.5 = (f32[3,1]{1,0:T(4,128)S(1)}, f32[3,1]{1,0:T(4,128)S(1)}, u32[]{:S(2)}, u32[]{:S(2)}) collective-permute-start(f32[3,1]{1,0:T(4,128)S(1)} %get-tuple-element.57), channel_id=1, source_target_pairs={{1,0},{2,1},{3,2},{4,3},{5,4},{6,5},{7,6},{8,7},{9,8},{10,9},{11,1... | collective-permute-start | bytes 44 | tf_op jit(solution)/shard_map/ppermute | solution.py:21
  658.3 1.0 copy-start.1
  659.4 42.6 %collective-permute-start.6 = (f32[3,1]{1,0:T(4,128)S(1)}, f32[3,1]{1,0:T(4,128)S(1)}, u32[]{:S(2)}, u32[]{:S(2)}) collective-permute-start(f32[3,1]{1,0:T(4,128)S(1)} %get-tuple-element.54), channel_id=1, source_target_pairs={{0,1},{1,2},{2,3},{3,4},{4,5},{5,6},{6,7},{7,8},{8,9},{9,10},{10,1... | collective-permute-start | bytes 44 | tf_op jit(solution)/shard_map/ppermute | solution.py:20
  661.3 40.7 %collective-permute-start.7 = (f32[3,1]{1,0:T(4,128)S(1)}, f32[3,1]{1,0:T(4,128)S(1)}, u32[]{:S(2)}, u32[]{:S(2)}) collective-permute-start(f32[3,1]{1,0:T(4,128)S(1)} %get-tuple-element.55), channel_id=1, source_target_pairs={{1,0},{2,1},{3,2},{4,3},{5,4},{6,5},{7,6},{8,7},{9,8},{10,9},{11,1... | collective-permute-start | bytes 44 | tf_op jit(solution)/shard_map/ppermute | solution.py:21
  (2 other events, 1.4 us)
Sparse Core Ops, SparseCore 0:
  60.4 54.1 reduce-scatter.15
  118.1 45.6 reduce-scatter.17
  210.5 52.0 reduce-scatter.19
  438.7 41.5 reduce-scatter.21
  659.4 41.5 reduce-scatter.23
where the time goes:
time: 850 us; the launch traced here: 842 us
  blocking collectives  462 us (54%)
  waiting for transfers between devices  156 us (18%)
  other arithmetic  100 us (12%)
  starting transfers between devices  60.5 us (7%)
  local copies, waits for them, and re-layouts  37.2 us (4%)
  between operations  25.2 us (3%)
    psum x3, blocking collectives, inner_pair(): return lax.psum((first, second), ('patch', 'elem'))  384 us
    unnamed x10, waiting for transfers between devices  156 us
    scatter-add x15, other arithmetic, scatter_rows(): accum = accum.at[:, inc[k]].add(values[3 * k:3 * k + 3])  95.8 us
    all_gather x3, blocking collectives, product(): whole = lax.all_gather(vec, 'elem', axis=1, tiled=True)  55.1 us
    ppermute x4, starting transfers between devices, padded_2(): after = lax.ppermute(first, axis, down)  50.7 us
    all_gather x1, blocking collectives, per_device(): whole_pos = lax.all_gather(positions, 'elem', axis=1, tiled=True)  22.9 us
  transfers between devices with their start and end apart: 13, of which 5 were waited for; matrix products, arithmetic and copies ran while one was open for 3% of the time, Pallas kernels for 0%

commit v1 on v0

v1 whole, which is shorter than its diff:
```python
import functools

import jax
import jax.numpy as jnp
from jax import lax
from jax.experimental import pallas as pl
from jax.experimental.pallas import tpu as pltpu
from jax.sharding import PartitionSpec as P

STIFF = 1.0
REG = 0.1
GROUPS = 8
LANES = 128
TRI_CHUNKS = 6
VERT_CHUNKS = 2
ROWS = VERT_CHUNKS * GROUPS
TRI_ROWS = TRI_CHUNKS * GROUPS

POS, TGT, INERTIA, COUNT, INC, RINV, RIM, PACKED = 0, 6, 12, 14, 16, 34, 58, 64

F32 = jnp.float32
BF16 = jnp.bfloat16


def vmem(n):
    return [pl.BlockSpec(memory_space=pltpu.VMEM)] * n


def iota(shape, axis):
    return lax.broadcasted_iota(jnp.int32, shape, axis)


def pack_kernel(pos, tgt, inertia, inc, rinv, counts, rim, out):
    first = lax.axis_index("elem") == 0
    out[0] = jnp.zeros((PACKED, LANES), F32)
    for k in range(VERT_CHUNKS):
        cut = slice(k * LANES, (k + 1) * LANES)
        out[0, POS + 3 * k : POS + 3 * k + 3] = pos[:, cut]
        out[0, TGT + 3 * k : TGT + 3 * k + 3] = tgt[:, cut]
        out[0, INERTIA + k : INERTIA + k + 1] = inertia[:, cut]
    out[0, COUNT : COUNT + 1] = jnp.full((1, LANES), counts[0], jnp.int32).astype(F32)
    for k in range(TRI_CHUNKS):
        cut = slice(k * LANES, (k + 1) * LANES)
        out[0, INC + 3 * k : INC + 3 * k + 3] = inc[:, cut].astype(F32)
        out[0, RINV + 4 * k : RINV + 4 * k + 4] = rinv[:, cut]
    out[0, RIM : RIM + 3] = jnp.where(first, rim[:, LANES:], rim[:, :LANES])
    block = out[0]
    for e in range(1, GROUPS):
        out[e] = block


def lane_rows(ref, row):
    return ref[pl.ds(row, GROUPS, stride=PACKED), :]


def corner_of(whole, k, q):
    index = lane_rows(whole, INC + 3 * k + q).astype(jnp.int32)
    row = ((index >> 7) & 1) * GROUPS + (index >> 8)
    return row, index & (LANES - 1)


def valid_of(whole, k):
    slot = iota((GROUPS, LANES), 1) + k * LANES
    return (slot.astype(F32) < lane_rows(whole, COUNT)).astype(F32)


def gather(field, row, lane):
    found = [jnp.zeros((GROUPS, LANES), F32)] * 3
    for h in range(ROWS):
        here = row == h
        for c in range(3):
            line = jnp.broadcast_to(field[c * ROWS + h : c * ROWS + h + 1, :], (GROUPS, LANES))
            value = jnp.take_along_axis(line, lane, axis=1, mode="promise_in_bounds")
            found[c] = jnp.where(here, value, found[c])
    return found


def scatter(values, row, lane, stage):
    comps = len(values)
    stage[0:8] = row.astype(F32)
    stage[8:16] = lane.astype(F32)
    for c, value in enumerate(values):
        upper = value.astype(BF16).astype(F32)
        stage[16 + 8 * c : 24 + 8 * c] = upper
        stage[16 + 8 * (comps + c) : 24 + 8 * (comps + c)] = value - upper
    rows_of = iota((ROWS, LANES), 0).astype(F32)
    lanes_of = iota((LANES, LANES), 0).astype(F32)
    left, right = [], []
    for e in range(GROUPS):
        def line(at, count):
            return jnp.broadcast_to(stage[at + e : at + e + 1, :], (count, LANES))
        here = line(0, ROWS) == rows_of
        left.append(jnp.concatenate(
            [jnp.where(here, line(16 + 8 * c, ROWS), 0.0).astype(BF16) for c in range(2 * comps)], axis=0))
        right.append(jnp.where(line(8, LANES) == lanes_of, 1.0, 0.0).astype(BF16))
    return lax.dot_general(
        jnp.concatenate(left, axis=1), jnp.concatenate(right, axis=1),
        (((1,), (1,)), ((), ())), preferred_element_type=F32)


def chain(here, before=None, after=None):
    lane = iota((GROUPS, LANES), 1)
    sub = iota((GROUPS, LANES), 0)
    low, high = here
    low_up, high_up = pltpu.roll(low, 1, 1), pltpu.roll(high, 1, 1)
    low_down, high_down = pltpu.roll(low, LANES - 1, 1), pltpu.roll(high, LANES - 1, 1)
    edge = 0.0 if before is None else pltpu.roll(jnp.broadcast_to(before, (GROUPS, LANES)), 1, 1)
    rim = jnp.where(sub == 0, edge, pltpu.roll(high_up, 1, 0))
    before_low = jnp.where(lane == 0, rim, low_up)
    before_high = jnp.where(lane == 0, low_up, high_up)
    edge = 0.0 if after is None else pltpu.roll(jnp.broadcast_to(after, (GROUPS, LANES)), LANES - 1, 1)
    rim = jnp.where(sub == GROUPS - 1, edge, pltpu.roll(low_down, GROUPS - 1, 0))
    after_low = jnp.where(lane == LANES - 1, high_down, low_down)
    after_high = jnp.where(lane == LANES - 1, rim, high_down)
    return (STIFF * (2.0 * low - before_low - after_low), STIFF * (2.0 * high - before_high - after_high))


def chunks(ref, c):
    at = c * ROWS
    return ref[at : at + GROUPS, :], ref[at + GROUPS : at + ROWS, :]


def put(ref, c, pair):
    at = c * ROWS
    ref[at : at + GROUPS, :] = pair[0]
    ref[at + GROUPS : at + ROWS, :] = pair[1]


def elements(whole, factors, field, stage, total):
    total[0 : 6 * ROWS] = jnp.zeros((6 * ROWS, LANES), F32)

    @pl.loop(0, TRI_CHUNKS)
    def _(k):
        places = [corner_of(whole, k, q) for q in range(3)]
        u = []
        for row, lane in places:
            u += gather(field, row, lane)

        def factor(j, m):
            return factors[pl.ds(pl.multiple_of((9 * j + m) * TRI_ROWS + k * GROUPS, GROUPS), GROUPS), :]

        inner = [sum(factor(j, m) * u[j] for j in range(9)) * (1.0 / 9.0) for m in range(9)]
        shift = REG * valid_of(whole, k)
        out = [sum(factor(j, m) * inner[m] for m in range(9)) + shift * u[j] for j in range(9)]
        part = 0.0
        for q, (row, lane) in enumerate(places):
            part += scatter(out[3 * q : 3 * q + 3], row, lane, stage)
        total[0 : 6 * ROWS] += part

    total[0 : 3 * ROWS] = total[0 : 3 * ROWS] + total[3 * ROWS : 6 * ROWS]


def inertia_of(whole):
    return [lane_rows(whole, INERTIA + k) for k in range(VERT_CHUNKS)]


def apply_local(whole, factors, field, stage, total, befores=None, afters=None):
    elements(whole, factors, field, stage, total)
    mass = inertia_of(whole)
    out = []
    for c in range(3):
        v = chunks(field, c)
        bent = chain(v, befores and befores[c], afters and afters[c])
        felt = chunks(total, c)
        out.append([mass[k] * v[k] + bent[k] + felt[k] for k in range(VERT_CHUNKS)])
    return out


def setup_kernel(whole, w_in, w_hid1, w_hid2, w_out, factors, first, image, diagonal, up, down,
                 pos, feats, w_first, w_last, raw, stage, total):
    for c in range(3):
        put(pos, c, [lane_rows(whole, POS + 3 * k + c) for k in range(VERT_CHUNKS)])
    feats[...] = jnp.zeros_like(feats)
    w_first[...] = jnp.zeros_like(w_first)
    w_first[:, 0:6] = w_in[...].astype(F32)
    w_last[...] = jnp.zeros_like(w_last)
    w_last[0:90, :] = w_out[...].astype(F32)
    w1 = w_first[...].astype(BF16)
    w4 = w_last[...].astype(BF16)
    total[...] = jnp.zeros_like(total)

    @pl.loop(0, TRI_CHUNKS)
    def _(k):
        places = [corner_of(whole, k, q) for q in range(3)]
        x0, x1, x2 = [gather(pos, row, lane) for row, lane in places]
        a, b, c_, d = [lane_rows(whole, RINV + 4 * k + i) for i in range(4)]
        for c in range(3):
            one, two = x1[c] - x0[c], x2[c] - x0[c]
            feats[pl.ds(c, GROUPS, stride=16), :] = one * a + two * c_
            feats[pl.ds(3 + c, GROUPS, stride=16), :] = one * b + two * d
        x = jnp.concatenate([feats[16 * e : 16 * e + 16, :] for e in range(GROUPS)], axis=1).astype(BF16)
        h = jnp.tanh(jnp.dot(w1, x, preferred_element_type=F32)).astype(BF16)
        h = jnp.tanh(jnp.dot(w_hid1[...], h, preferred_element_type=F32)).astype(BF16)
        h = jnp.tanh(jnp.dot(w_hid2[...], h, preferred_element_type=F32)).astype(BF16)
        o = jnp.dot(w4, h, preferred_element_type=F32)
        for e in range(GROUPS):
            for g in range(12):
                raw[pl.ds(g * 64 + e, 8, stride=8), :] = o[8 * g : 8 * g + 8, e * LANES : (e + 1) * LANES]
        valid = valid_of(whole, k)
        forces, curves = [], []
        for j in range(9):
            forces.append(raw[8 * j : 8 * j + 8, :] * valid)
            curve = 0.0
            for m in range(9):
                at = 9 * j + m
                g = (raw[8 * (9 + at) : 8 * (9 + at) + 8, :] * valid).astype(BF16).astype(F32)
                factors[pl.ds(pl.multiple_of(at * TRI_ROWS + k * GROUPS, GROUPS), GROUPS), :] = g
                curve += g * g
            curves.append(curve * (1.0 / 9.0) + REG * valid)
        part = 0.0
        for q, (row, lane) in enumerate(places):
            part += scatter(forces[3 * q : 3 * q + 3] + curves[3 * q : 3 * q + 3], row, lane, stage)
        total[...] += part

    total[0 : 6 * ROWS] = total[0 : 6 * ROWS] + total[6 * ROWS : 12 * ROWS]
    mass = inertia_of(whole)
    inverse = []
    for c in range(3):
        x = chunks(pos, c)
        bent = chain(x, whole[RIM + c : RIM + c + 1, :],
                     whole[(GROUPS - 1) * PACKED + RIM + c : (GROUPS - 1) * PACKED + RIM + c + 1, :])
        felt, curve = chunks(total, c), chunks(total, 3 + c)
        diag = [mass[k] + curve[k] + 2.0 * STIFF for k in range(VERT_CHUNKS)]
        inv = [1.0 / diag[k] for k in range(VERT_CHUNKS)]
        grad = [mass[k] * (x[k] - lane_rows(whole, TGT + 3 * k + c)) + bent[k] + felt[k]
                for k in range(VERT_CHUNKS)]
        put(diagonal, c, diag)
        put(first, c, [-grad[k] * inv[k] for k in range(VERT_CHUNKS)])
        inverse.append(inv)
    w = apply_local(whole, factors, first, stage, total)
    up[...] = jnp.zeros_like(up)
    down[...] = jnp.zeros_like(down)
    for c in range(3):
        v = chunks(first, c)
        put(image, c, w[c])
        nxt = [w[c][k] * inverse[c][k] - v[k] for k in range(VERT_CHUNKS)]
        for i, what in enumerate((v, nxt, inverse[c])):
            up[3 * i + c : 3 * i + c + 1, :] = what[1][GROUPS - 1 : GROUPS, :]
            down[3 * i + c : 3 * i + c + 1, :] = what[0][0:1, :]


def krylov_kernel(whole, factors, first, image, diagonal, above, below,
                  second, third, last_image, sums, stage, total):
    lane = iota((GROUPS, LANES), 1)
    sub = iota((GROUPS, LANES), 0)
    head = (lane == 0) & (sub == 0)
    tail = (lane == LANES - 1) & (sub == GROUPS - 1)

    def spread(row):
        return jnp.broadcast_to(row, (GROUPS, LANES))

    befores, afters = [], []
    for c in range(3):
        v0, w0 = chunks(first, c), chunks(image, c)
        diag = chunks(diagonal, c)
        inv = [1.0 / diag[k] for k in range(VERT_CHUNKS)]
        old_up, old_down = above[c : c + 1, :], below[c : c + 1, :]
        w_low = w0[0] - STIFF * jnp.where(head, pltpu.roll(spread(old_up), 1, 1), 0.0)
        w_high = w0[1] - STIFF * jnp.where(tail, pltpu.roll(spread(old_down), LANES - 1, 1), 0.0)
        put(second, c, [w_low * inv[0] - v0[0], w_high * inv[1] - v0[1]])
        mine_low = pltpu.roll(spread(v0[0][0:1, :]), LANES - 1, 1)[0:1, :]
        mine_high = pltpu.roll(spread(v0[1][GROUPS - 1 : GROUPS, :]), 1, 1)[0:1, :]
        befores.append(above[3 + c : 4 + c, :] - STIFF * mine_low * above[6 + c : 7 + c, :])
        afters.append(below[3 + c : 4 + c, :] - STIFF * mine_high * below[6 + c : 7 + c, :])
    w = apply_local(whole, factors, second, stage, total, befores, afters)
    for c in range(3):
        diag, v1 = chunks(diagonal, c), chunks(second, c)
        put(third, c, [w[c][k] / diag[k] - v1[k] for k in range(VERT_CHUNKS)])
    w = apply_local(whole, factors, third, stage, total)
    moment = [0.0] * 6
    ends = []
    for c in range(3):
        put(last_image, c, w[c])
        diag = chunks(diagonal, c)
        v0, v1, v2 = chunks(first, c), chunks(second, c), chunks(third, c)
        for k in range(VERT_CHUNKS):
            m0, m1, m2 = diag[k] * v0[k], diag[k] * v1[k], diag[k] * v2[k]
            for i, term in enumerate((m0 * v0[k], m0 * v1[k], m1 * v1[k], m1 * v2[k], m2 * v2[k],
                                      v2[k] * w[c][k] - m2 * v2[k])):
                moment[i] += term
        ends.append((jnp.where(head, v2[0], 0.0), jnp.where(tail, v2[1], 0.0)))
    line = jnp.zeros((1, LANES), F32)
    for i, part in enumerate(moment + [x[0] for x in ends] + [x[1] for x in ends]):
        value = jnp.sum(jnp.sum(part, axis=0, keepdims=True), axis=1, keepdims=True)
        line = jnp.where(iota((1, LANES), 1) == i, value, line)
    sums[...] = jnp.broadcast_to(line, sums.shape)


def finish_kernel(sums, first, second, third, last_image, diagonal, field, residual):
    patch, elem = lax.axis_index("patch"), lax.axis_index("elem")
    patches = sums.shape[0]
    every = sums[...]
    lane = iota(every.shape, 1)
    sub = iota(every.shape, 0)
    totals = jnp.sum(every, axis=0, keepdims=True)

    def pick(row, i):
        return jnp.sum(jnp.where(iota((1, LANES), 1) == i, row, 0.0), axis=1, keepdims=True)

    after = pltpu.roll(pltpu.roll(every, patches - 1, 0), 3, 1)
    coupled = jnp.where((lane >= 9) & (lane < 12) & (sub < patches - 1), every * after, 0.0)
    coupling = jnp.sum(jnp.sum(coupled, axis=0, keepdims=True), axis=1, keepdims=True)
    mu = [pick(totals, i) for i in range(6)]
    mu[5] = mu[5] - 2.0 * STIFF * coupling

    def inner(p, q):
        return sum(a * b * mu[i + j] for i, a in enumerate(p) for j, b in enumerate(q))

    def applied(p):
        padded = list(p) + [0.0 * mu[0]]
        return [padded[0]] + [padded[j] + padded[j - 1] for j in range(1, len(padded))]

    one = jnp.ones((1, 1), F32)
    z, direction, x = [one], [one], []
    rz = inner(z, z)
    for step in range(3):
        ahead = applied(direction)
        alpha = rz / inner(direction, ahead)
        x = [(x[j] if j < len(x) else 0.0) + alpha * direction[j] for j in range(len(direction))]
        z = [(z[j] if j < len(z) else 0.0) - alpha * ahead[j] for j in range(len(ahead))]
        if step < 2:
            new = inner(z, z)
            ratio = new / rz
            direction = [z[j] + (ratio * direction[j] if j < len(direction) else 0.0) for j in range(len(z))]
            rz = new
    place = iota((1, LANES), 1)
    prev = sums[pl.ds(jnp.maximum(patch - 1, 0), 1), :]
    nxt = sums[pl.ds(jnp.minimum(patch + 1, patches - 1), 1), :]
    at_head = (place == 0) & (elem == 0) & (patch > 0)
    at_tail = (place == LANES - 1) & (elem == GROUPS - 1) & (patch < patches - 1)
    for c in range(3):
        for k in range(VERT_CHUNKS):
            at = pl.ds(c * ROWS + k * GROUPS + elem, 1)
            v0, v1, v2, w2, diag = first[at, :], second[at, :], third[at, :], last_image[at, :], diagonal[at, :]
            if k == 0:
                w2 = w2 - STIFF * jnp.where(at_head, pick(prev, 9 + c), 0.0)
            else:
                w2 = w2 - STIFF * jnp.where(at_tail, pick(nxt, 6 + c), 0.0)
            v3 = w2 / diag - v2
            cut = slice(k * LANES, (k + 1) * LANES)
            field[c : c + 1, cut] = x[0] * v0 + x[1] * v1 + x[2] * v2
            residual[c : c + 1, cut] = diag * (z[0] * v0 + z[1] * v1 + z[2] * v2 + z[3] * v3)


def shape(*dims):
    return jax.ShapeDtypeStruct(dims, F32)


def per_device(positions, target, inertia, incidence, rest_inverse, counts, w_in, w_hid1, w_hid2, w_out):
    patches = lax.axis_size("patch")
    params = pltpu.CompilerParams(vmem_limit_bytes=48 * 1024 * 1024)
    swaps = []
    for p in range(patches - 1):
        left, right = p * GROUPS + GROUPS - 1, (p + 1) * GROUPS
        swaps += [(left, right), (right, left)]
    rim = lax.ppermute(positions, ("patch", "elem"), swaps)
    packed = pl.pallas_call(
        pack_kernel, out_shape=shape(GROUPS, PACKED, LANES),
        in_specs=vmem(5) + [pl.BlockSpec(memory_space=pltpu.SMEM)] + vmem(1), out_specs=vmem(1)[0],
        name="pack",
    )(positions, target, inertia, incidence, rest_inverse, counts, rim)
    whole = lax.all_to_all(packed, "elem", 0, 0, tiled=True).reshape(GROUPS * PACKED, LANES)
    wide = 3 * ROWS
    factors, first, image, diagonal, up, down = pl.pallas_call(
        setup_kernel,
        out_shape=[shape(81 * TRI_ROWS, LANES), shape(wide, LANES), shape(wide, LANES), shape(wide, LANES),
                   shape(16, LANES), shape(16, LANES)],
        in_specs=vmem(5), out_specs=vmem(6),
        scratch_shapes=[pltpu.VMEM((wide, LANES), F32), pltpu.VMEM((GROUPS * 16, LANES), F32),
                        pltpu.VMEM((LANES, 16), F32), pltpu.VMEM((96, LANES), F32),
                        pltpu.VMEM((96 * GROUPS, LANES), F32), pltpu.VMEM((14 * GROUPS, LANES), F32),
                        pltpu.VMEM((12 * ROWS, LANES), F32)],
        compiler_params=params, name="setup",
    )(whole, w_in, w_hid1, w_hid2, w_out)
    above = lax.ppermute(up, "patch", [(p, p + 1) for p in range(patches - 1)])
    below = lax.ppermute(down, "patch", [(p + 1, p) for p in range(patches - 1)])
    second, third, last_image, sums = pl.pallas_call(
        krylov_kernel,
        out_shape=[shape(wide, LANES), shape(wide, LANES), shape(wide, LANES), shape(patches, LANES)],
        in_specs=vmem(7), out_specs=vmem(4),
        scratch_shapes=[pltpu.VMEM((8 * GROUPS, LANES), F32), pltpu.VMEM((6 * ROWS, LANES), F32)],
        compiler_params=params, name="krylov",
    )(whole, factors, first, image, diagonal, above, below)
    sums = lax.all_to_all(sums, "patch", 0, 0, tiled=True)
    return pl.pallas_call(
        finish_kernel, out_shape=[shape(*positions.shape)] * 2,
        in_specs=vmem(6), out_specs=vmem(2), compiler_params=params, name="finish",
    )(sums, first, second, third, last_image, diagonal)


def solution(mesh):
    split = P(None, ("patch", "elem"))
    placed = (split,) * 5 + (P(("patch", "elem")),) + (P(),) * 4
    return jax.shard_map(per_device, mesh=mesh, in_specs=placed, out_specs=(split, split), check_vma=False)
```

time: 850 us -> 105 us (0.12)
  blocking collectives: 462 us -> 40.8 us
  waiting for transfers between devices: 156 us -> 10.2 us
  other arithmetic: 100 us -> 0 us
  starting transfers between devices: 60.5 us -> 21.6 us
  local copies, waits for them, and re-layouts: 37.2 us -> 3.65 us
  Pallas kernels: 0 us -> 26.6 us
  between operations: 25.2 us -> 1.32 us
    psum x3 -> x0, blocking collectives: 384 us -> none  [inner_pair(): return lax.psum((first, second), ('patch', 'elem'))]
    unnamed x10 -> x0, waiting for transfers between devices: 156 us -> none
    scatter-add x15 -> x0, other arithmetic: 95.8 us -> none  [scatter_rows(): accum = accum.at[:, inc[k]].add(values[3 * k:3 * k + 3])]
    all_gather x4 -> x0, blocking collectives: 78 us -> none  [the longest x3 55.1 us: product(): whole = lax.all_gather(vec, 'elem', axis=1, tiled=True)]
    ppermute x8 -> x3, starting transfers between devices: 60.1 us -> 17.1 us  [the longest x1 6.5 us: per_device(): above = lax.ppermute(up, 'patch', [(p, p + 1) for p in range(patches - 1)])]
    all_to_all x0 -> x1, blocking collectives: none -> 40.8 us  [per_device(): sums = lax.all_to_all(sums, 'patch', 0, 0, tiled=True)]
    pallas_call x0 -> x4, Pallas kernels: none -> 26.6 us  [the longest x1 14.5 us: per_device(): pl.pallas_call(setup_kernel, out_shape=[shape(81 * TRI_ROWS, LANES), shap...]
    gather x24 -> x0, local copies, waits for them, and re-layouts: 20.7 us -> none  [the longest x18 15.6 us: tri_apply(): gathered = jnp.concatenate([vec[:, inc[k]] for k in range(3)], axis=0)]
  transfers between devices with their start and end apart: 13 -> 4, of which waited for: 5 -> 3; matrix products, arithmetic and copies ran while one was open for 3% -> 1% of each run, Pallas kernels for 0% -> 0%
where the time goes in v1:
time: 105 us; the launch traced here: 104 us
  blocking collectives  40.8 us (39%)
  Pallas kernels  26.6 us (25%)
  starting transfers between devices  21.6 us (21%)
  waiting for transfers between devices  10.2 us (10%)
  local copies, waits for them, and re-layouts  3.65 us (3%)
  between operations  1.32 us (1%)
    all_to_all x1, blocking collectives, per_device(): sums = lax.all_to_all(sums, 'patch', 0, 0, tiled=True)  40.8 us
    pallas_call x1, Pallas kernels, per_device(): pl.pallas_call(setup_kernel, out_shape=[shape(81 * TRI_ROWS, LANES), shap...  14.5 us
    pallas_call x1, Pallas kernels, per_device(): pl.pallas_call(krylov_kernel, out_shape=[shape(wide, LANES), shape(wide,...  9.73 us
    all_to_all x1, waiting for transfers between devices, per_device(): lax.all_to_all(packed, 'elem', 0, 0, tiled=True)  8.52 us
    ppermute x1, starting transfers between devices, per_device(): above = lax.ppermute(up, 'patch', [(p, p + 1) for p in range(patches - 1)])  6.5 us
    ppermute x1, starting transfers between devices, per_device(): rim = lax.ppermute(positions, ('patch', 'elem'), swaps)  6.49 us
    all_to_all x1, starting transfers between devices, per_device(): lax.all_to_all(packed, 'elem', 0, 0, tiled=True)  4.59 us
    ppermute x1, starting transfers between devices, per_device(): lax.ppermute(down, 'patch', [(p + 1, p) for p in range(patches - 1)])  4.08 us
  transfers between devices with their start and end apart: 4, of which 3 were waited for; matrix products, arithmetic and copies ran while one was open for 1% of the time, Pallas kernels for 0%

profile of v1, /device:TPU:1, one launch (start us, length us, event | category | flops | bytes accessed | tf_op | source)
XLA Modules:
  0.0 104.2 jit_solution(9878730590130654479)
XLA Ops:
  0.6 6.5 %collective-permute-start = (f32[3,256]{1,0:T(4,128)}, f32[3,256]{1,0:T(4,128)S(1)}, u32[]{:S(2)}, u32[]{:S(2)}) collective-permute-start(f32[3,256]{1,0:T(4,128)} %pos.1), channel_id=1, source_target_pairs={{7,8},{8,7},{15,16},{16,15},{23,24},{24,23},{31,32},{32,31},{39,40... | collective-permute-start | bytes 9224 | tf_op jit(solution)/shard_map/ppermute | solution.py:356
  7.8 0.8 collective-permute-done.rim
  8.6 0.0 copy-start.3
  8.6 0.6 copy-done.3
  9.2 1.5 %pack.1 = f32[8,64,128]{2,1,0:T(8,128)} custom-call(f32[3,256]{1,0:T(4,128)} %pos.1, f32[3,256]{1,0:T(4,128)} %tgt.1, f32[1,256]{1,0:T(1,128)} %inertia.1, s32[3,768]{1,0:T(4,128)} %inc.1, f32[4,768]{1,0:T(4,128)} %rinv.1, s32[1]{0:T(128)S(6)} %copy.15.counts, f32[3,256]{1,0:T(4,128)} %copy-done.3), custom_call_target="tpu_custom_call" | custom-call | tf_op jit(solution)/shard_map/pack/pallas_call | solution.py:357
  10.7 4.6 %all-to-all-start = ((f32[8,64,128]{2,1,0:T(8,128)}), f32[8,64,128]{2,1,0:T(8,128)S(1)}, u32[]{:S(2)}, u32[]{:S(2)}) async-start(f32[8,64,128]{2,1,0:T(8,128)} %pack.1), calls=%async_computation | async-start | bytes 524288 | tf_op jit(solution)/shard_map/all_to_all | solution.py:362
  15.3 0.8 copy.13.w_in
  16.1 8.5 %all-to-all-done = f32[8,64,128]{2,1,0:T(8,128)S(1)} async-done(((f32[8,64,128]{2,1,0:T(8,128)}), f32[8,64,128]{2,1,0:T(8,128)S(1)}, u32[]{:S(2)}, u32[]{:S(2)}) %all-to-all-start) | async-done | bytes 262176 | tf_op jit(solution)/shard_map/all_to_all | solution.py:362
  24.6 0.0 copy-start
  24.6 0.8 copy-done
  25.4 0.0 copy-start.1
  25.4 0.8 copy-done.1
  26.2 0.0 copy-start.2
  26.2 0.7 copy-done.2
  26.9 14.5 %setup.1 = (f32[3888,128]{1,0:T(8,128)S(1)}, f32[48,128]{1,0:T(8,128)S(1)}, f32[48,128]{1,0:T(8,128)S(1)}, f32[48,128]{1,0:T(8,128)S(1)}, f32[16,128]{1,0:T(8,128)S(1)}, /*index=5*/f32[16,128]{1,0:T(8,128)S(1)}) custom-call(f32[512,128]{1,0:T(8,128)S(1)} %bitcast.5, bf16[128,6]{1,0:T(8,128)(2,1)S(1)} %copy.13.w_in, bf16[128,128]{1,0:T(8,128)(2,1)S(1)} %copy-done, ...), custom_call_target="tpu_custom_call" | custom-call | tf_op jit(solution)/shard_map/setup/pallas_call | solution.py:364
  41.4 6.5 %collective-permute-start.1 = (f32[16,128]{1,0:T(8,128)S(1)}, f32[16,128]{1,0:T(8,128)S(1)}, u32[]{:S(2)}, u32[]{:S(2)}) collective-permute-start(f32[16,128]{1,0:T(8,128)S(1)} %get-tuple-element.16), channel_id=1, source_target_pairs={{0,8},{8,16},{16,24},{24,32},{32,40},{40,48},{48,56},{56,64},{64,7... | collective-permute-start | bytes 24584 | tf_op jit(solution)/shard_map/ppermute | solution.py:375
  47.9 4.1 %collective-permute-start.2 = (f32[16,128]{1,0:T(8,128)S(1)}, f32[16,128]{1,0:T(8,128)S(1)}, u32[]{:S(2)}, u32[]{:S(2)}) collective-permute-start(f32[16,128]{1,0:T(8,128)S(1)} %get-tuple-element.17), channel_id=1, source_target_pairs={{8,0},{16,8},{24,16},{32,24},{40,32},{48,40},{56,48},{64,56},{72,6... | collective-permute-start | bytes 24584 | tf_op jit(solution)/shard_map/ppermute | solution.py:376
  52.0 0.0 collective-permute-done.1.above
  52.0 0.9 collective-permute-done.2.below
  52.9 9.7 %krylov.1 = (f32[48,128]{1,0:T(8,128)S(1)}, f32[48,128]{1,0:T(8,128)S(1)}, f32[48,128]{1,0:T(8,128)S(1)}, f32[128,128]{1,0:T(8,128)S(1)}) custom-call(f32[512,128]{1,0:T(8,128)S(1)} %bitcast.6, f32[3888,128]{1,0:T(8,128)S(1)} %get-tuple-element.12.factors, f32[48,128]{1,0:T(8,128)S(1)} %get-tuple-element.13.first, f32[48,128]{1,0:T(8,128)S(1)} %get-tuple-element.14.image, ...), custom_call_target="tpu_custom_call" | custom-call | tf_op jit(solution)/shard_map/krylov/pallas_call | solution.py:377
  62.6 40.8 %all_to_all.16 = f32[128,1,128]{2,1,0:T(1,128)S(1)} all-to-all(f32[128,1,128]{2,1,0:T(1,128)S(1)} %bitcast.8), channel_id=1, replica_groups=mesh['patch'=128,'elem'=8] {'patch'}, dimensions={0} | all-to-all | bytes 131072 | tf_op jit(solution)/shard_map/all_to_all | solution.py:384
  103.4 0.8 finish.1
Async XLA Ops:
  0.6 8.0 %collective-permute-start = (f32[3,256]{1,0:T(4,128)}, f32[3,256]{1,0:T(4,128)S(1)}, u32[]{:S(2)}, u32[]{:S(2)}) collective-permute-start(f32[3,256]{1,0:T(4,128)} %pos.1), channel_id=1, source_target_pairs={{7,8},{8,7},{15,16},{16,15},{23,24},{24,23},{31,32},{32,31},{39,40... | collective-permute-start | bytes 9224 | tf_op jit(solution)/shard_map/ppermute | solution.py:356
  8.6 0.6 copy-start.3
  10.7 13.9 %all-to-all-start = ((f32[8,64,128]{2,1,0:T(8,128)}), f32[8,64,128]{2,1,0:T(8,128)S(1)}, u32[]{:S(2)}, u32[]{:S(2)}) async-start(f32[8,64,128]{2,1,0:T(8,128)} %pack.1), calls=%async_computation | async-start | bytes 524288 | tf_op jit(solution)/shard_map/all_to_all | solution.py:362
  24.6 0.8 copy-start
  25.4 0.8 copy-start.1
  26.2 0.7 copy-start.2
  41.4 10.6 %collective-permute-start.1 = (f32[16,128]{1,0:T(8,128)S(1)}, f32[16,128]{1,0:T(8,128)S(1)}, u32[]{:S(2)}, u32[]{:S(2)}) collective-permute-start(f32[16,128]{1,0:T(8,128)S(1)} %get-tuple-element.16), channel_id=1, source_target_pairs={{0,8},{8,16},{16,24},{24,32},{32,40},{40,48},{48,56},{56,64},{64,7... | collective-permute-start | bytes 24584 | tf_op jit(solution)/shard_map/ppermute | solution.py:375
  47.9 5.0 %collective-permute-start.2 = (f32[16,128]{1,0:T(8,128)S(1)}, f32[16,128]{1,0:T(8,128)S(1)}, u32[]{:S(2)}, u32[]{:S(2)}) collective-permute-start(f32[16,128]{1,0:T(8,128)S(1)} %get-tuple-element.17), channel_id=1, source_target_pairs={{8,0},{16,8},{24,16},{32,24},{40,32},{48,40},{56,48},{64,56},{72,6... | collective-permute-start | bytes 24584 | tf_op jit(solution)/shard_map/ppermute | solution.py:376

commit v2 on v1

--- a/solution.py
+++ b/solution.py
@@ -18,6 +18,8 @@
 
 POS, TGT, INERTIA, COUNT, INC, RINV, RIM, PACKED = 0, 6, 12, 14, 16, 34, 58, 64
 
+HID1, HID2, LAST, WEIGHTS = 16, 144, 272, 368
+
 F32 = jnp.float32
 BF16 = jnp.bfloat16
 
@@ -30,8 +32,12 @@
     return lax.broadcasted_iota(jnp.int32, shape, axis)
 
 
-def pack_kernel(pos, tgt, inertia, inc, rinv, counts, rim, out):
+def pack_kernel(pos, tgt, inertia, inc, rinv, counts, w_in, w_hid1, w_hid2, w_out, rim, out, weights):
     first = lax.axis_index("elem") == 0
+    weights[0:16] = jnp.concatenate([w_in[...].astype(F32), jnp.zeros((10, LANES), F32)], axis=0).astype(BF16)
+    weights[HID1:HID2] = w_hid1[...]
+    weights[HID2:LAST] = w_hid2[...]
+    weights[LAST:WEIGHTS] = jnp.concatenate([w_out[...].astype(F32), jnp.zeros((6, LANES), F32)], axis=0).astype(BF16)
     out[0] = jnp.zeros((PACKED, LANES), F32)
     for k in range(VERT_CHUNKS):
         cut = slice(k * LANES, (k + 1) * LANES)
@@ -64,38 +70,63 @@
     return (slot.astype(F32) < lane_rows(whole, COUNT)).astype(F32)
 
 
-def gather(field, row, lane):
-    found = [jnp.zeros((GROUPS, LANES), F32)] * 3
+def one_hot(row, lane, q, k, hot_lane, hot_row, stage):
+    stage[0:8] = row.astype(F32)
+    stage[8:16] = lane.astype(F32)
+    places = iota((LANES, LANES), 0).astype(F32)
+    for e in range(GROUPS):
+        at = q * GROUPS * LANES + e * LANES
+        for ref, first, count in ((hot_row, e, ROWS), (hot_lane, 8 + e, LANES)):
+            line = jnp.broadcast_to(stage[first : first + 1, :], (count, LANES))
+            ref[k, :, at : at + LANES] = jnp.where(line == places[:count], 1.0, 0.0).astype(BF16)
+
+
+def gather(field, places):
+    found = [[jnp.zeros((GROUPS, LANES), F32)] * 3 for _ in places]
     for h in range(ROWS):
-        here = row == h
+        here = [row == h for row, _ in places]
         for c in range(3):
             line = jnp.broadcast_to(field[c * ROWS + h : c * ROWS + h + 1, :], (GROUPS, LANES))
-            value = jnp.take_along_axis(line, lane, axis=1, mode="promise_in_bounds")
-            found[c] = jnp.where(here, value, found[c])
+            for q, (_, lane) in enumerate(places):
+                value = jnp.take_along_axis(line, lane, axis=1, mode="promise_in_bounds")
+                found[q][c] = jnp.where(here[q], value, found[q][c])
     return found
 
 
-def scatter(values, row, lane, stage):
-    comps = len(values)
-    stage[0:8] = row.astype(F32)
-    stage[8:16] = lane.astype(F32)
-    for c, value in enumerate(values):
-        upper = value.astype(BF16).astype(F32)
-        stage[16 + 8 * c : 24 + 8 * c] = upper
-        stage[16 + 8 * (comps + c) : 24 + 8 * (comps + c)] = value - upper
-    rows_of = iota((ROWS, LANES), 0).astype(F32)
-    lanes_of = iota((LANES, LANES), 0).astype(F32)
-    left, right = [], []
-    for e in range(GROUPS):
-        def line(at, count):
-            return jnp.broadcast_to(stage[at + e : at + e + 1, :], (count, LANES))
-        here = line(0, ROWS) == rows_of
-        left.append(jnp.concatenate(
-            [jnp.where(here, line(16 + 8 * c, ROWS), 0.0).astype(BF16) for c in range(2 * comps)], axis=0))
-        right.append(jnp.where(line(8, LANES) == lanes_of, 1.0, 0.0).astype(BF16))
-    return lax.dot_general(
-        jnp.concatenate(left, axis=1), jnp.concatenate(right, axis=1),
-        (((1,), (1,)), ((), ())), preferred_element_type=F32)
+def spread_out(values, k, hot_row, stage, spread):
+    comps = len(values[0])
+    for q in range(3):
+        for c, value in enumerate(values[q]):
+            upper = value.astype(BF16).astype(F32)
+            stage[q, 8 * c : 8 * c + 8] = upper
+            stage[q, 8 * (comps + c) : 8 * (comps + c) + 8] = value - upper
+        for e in range(GROUPS):
+            at = q * GROUPS * LANES + e * LANES
+            mask = hot_row[k, :, at : at + LANES]
+            for c in range(2 * comps):
+                line = jnp.broadcast_to(stage[q, 8 * c + e : 8 * c + e + 1, :], (ROWS, LANES)).astype(BF16)
+                spread[ROWS * c : ROWS * (c + 1), at : at + LANES] = line * mask
+
+
+def collect(spread, k, hot_lane):
+    return lax.dot_general(spread[...], hot_lane[k], (((1,), (1,)), ((), ())), preferred_element_type=F32)
+
+
+def sweep(build, hot_lane, spreads, total):
+    total[...] = jnp.zeros_like(total)
+    spreads[1][...] = jnp.zeros_like(spreads[1])
+
+    @pl.loop(0, TRI_CHUNKS // 2)
+    def _(i):
+        for half in range(2):
+            k = 2 * i + half
+            part = collect(spreads[1 - half], jnp.maximum(k - 1, 0), hot_lane)
+            build(k, spreads[half])
+            total[...] += part
+
+    half = total.shape[0] // 2
+    whole = total[...] + collect(spreads[1], TRI_CHUNKS - 1, hot_lane)
+    total[0:half] = whole[:half] + whole[half:]
 
 
 def chain(here, before=None, after=None):
@@ -126,15 +157,10 @@
     ref[at + GROUPS : at + ROWS, :] = pair[1]
 
 
-def elements(whole, factors, field, stage, total):
-    total[0 : 6 * ROWS] = jnp.zeros((6 * ROWS, LANES), F32)
-
-    @pl.loop(0, TRI_CHUNKS)
-    def _(k):
-        places = [corner_of(whole, k, q) for q in range(3)]
-        u = []
-        for row, lane in places:
-            u += gather(field, row, lane)
+def elements(whole, factors, hot_lane, hot_row, field, stage, spreads, total):
+    def build(k, spread):
+        found = gather(field, [corner_of(whole, k, q) for q in range(3)])
+        u = found[0] + found[1] + found[2]
 
         def factor(j, m):
             return factors[pl.ds(pl.multiple_of((9 * j + m) * TRI_ROWS + k * GROUPS, GROUPS), GROUPS), :]
@@ -142,20 +168,17 @@
         inner = [sum(factor(j, m) * u[j] for j in range(9)) * (1.0 / 9.0) for m in range(9)]
         shift = REG * valid_of(whole, k)
         out = [sum(factor(j, m) * inner[m] for m in range(9)) + shift * u[j] for j in range(9)]
-        part = 0.0
-        for q, (row, lane) in enumerate(places):
-            part += scatter(out[3 * q : 3 * q + 3], row, lane, stage)
-        total[0 : 6 * ROWS] += part
-
-    total[0 : 3 * ROWS] = total[0 : 3 * ROWS] + total[3 * ROWS : 6 * ROWS]
+        spread_out([out[0:3], out[3:6], out[6:9]], k, hot_row, stage, spread)
+
+    sweep(build, hot_lane, spreads, total)
 
 
 def inertia_of(whole):
     return [lane_rows(whole, INERTIA + k) for k in range(VERT_CHUNKS)]
 
 
-def apply_local(whole, factors, field, stage, total, befores=None, afters=None):
-    elements(whole, factors, field, stage, total)
+def apply_local(whole, factors, hots, field, stage, spreads, total, befores=None, afters=None):
+    elements(whole, factors, *hots, field, stage, spreads, total)
     mass = inertia_of(whole)
     out = []
     for c in range(3):
@@ -166,36 +189,39 @@
     return out
 
 
-def setup_kernel(whole, w_in, w_hid1, w_hid2, w_out, factors, first, image, diagonal, up, down,
-                 pos, feats, w_first, w_last, raw, stage, total):
+def setup_kernel(whole, weights, factors, hot_lane, hot_row, first, image, diagonal, up, down,
+                 pos, feats, inputs, outputs, raw, stage6, spread6a, spread6b, total6,
+                 stage, spread_a, spread_b, total):
     for c in range(3):
         put(pos, c, [lane_rows(whole, POS + 3 * k + c) for k in range(VERT_CHUNKS)])
     feats[...] = jnp.zeros_like(feats)
-    w_first[...] = jnp.zeros_like(w_first)
-    w_first[:, 0:6] = w_in[...].astype(F32)
-    w_last[...] = jnp.zeros_like(w_last)
-    w_last[0:90, :] = w_out[...].astype(F32)
-    w1 = w_first[...].astype(BF16)
-    w4 = w_last[...].astype(BF16)
-    total[...] = jnp.zeros_like(total)
 
     @pl.loop(0, TRI_CHUNKS)
     def _(k):
         places = [corner_of(whole, k, q) for q in range(3)]
-        x0, x1, x2 = [gather(pos, row, lane) for row, lane in places]
+        for q, (row, lane) in enumerate(places):
+            one_hot(row, lane, q, k, hot_lane, hot_row, stage.at[q])
+        x0, x1, x2 = gather(pos, places)
         a, b, c_, d = [lane_rows(whole, RINV + 4 * k + i) for i in range(4)]
         for c in range(3):
             one, two = x1[c] - x0[c], x2[c] - x0[c]
             feats[pl.ds(c, GROUPS, stride=16), :] = one * a + two * c_
             feats[pl.ds(3 + c, GROUPS, stride=16), :] = one * b + two * d
-        x = jnp.concatenate([feats[16 * e : 16 * e + 16, :] for e in range(GROUPS)], axis=1).astype(BF16)
-        h = jnp.tanh(jnp.dot(w1, x, preferred_element_type=F32)).astype(BF16)
-        h = jnp.tanh(jnp.dot(w_hid1[...], h, preferred_element_type=F32)).astype(BF16)
-        h = jnp.tanh(jnp.dot(w_hid2[...], h, preferred_element_type=F32)).astype(BF16)
-        o = jnp.dot(w4, h, preferred_element_type=F32)
+        inputs[k] = jnp.concatenate([feats[16 * e : 16 * e + 16, :] for e in range(GROUPS)], axis=1).astype(BF16)
+
+    x = jnp.concatenate([inputs[k] for k in range(TRI_CHUNKS)], axis=1)
+    h = lax.dot_general(weights[0:HID1], x, (((0,), (0,)), ((), ())), preferred_element_type=F32)
+    h = jnp.tanh(h).astype(BF16)
+    for weight in (weights[HID1:HID2], weights[HID2:LAST]):
+        h = jnp.tanh(jnp.dot(weight, h, preferred_element_type=F32)).astype(BF16)
+    o = jnp.dot(weights[LAST:WEIGHTS], h, preferred_element_type=F32)
+    for k in range(TRI_CHUNKS):
+        outputs[k] = o[:, k * GROUPS * LANES : (k + 1) * GROUPS * LANES]
+
+    def build(k, spread):
         for e in range(GROUPS):
             for g in range(12):
-                raw[pl.ds(g * 64 + e, 8, stride=8), :] = o[8 * g : 8 * g + 8, e * LANES : (e + 1) * LANES]
+                raw[pl.ds(g * 64 + e, 8, stride=8), :] = outputs[k, 8 * g : 8 * g + 8, e * LANES : (e + 1) * LANES]
         valid = valid_of(whole, k)
         forces, curves = [], []
         for j in range(9):
@@ -207,19 +233,17 @@
                 factors[pl.ds(pl.multiple_of(at * TRI_ROWS + k * GROUPS, GROUPS), GROUPS), :] = g
                 curve += g * g
             curves.append(curve * (1.0 / 9.0) + REG * valid)
-        part = 0.0
-        for q, (row, lane) in enumerate(places):
-            part += scatter(forces[3 * q : 3 * q + 3] + curves[3 * q : 3 * q + 3], row, lane, stage)
-        total[...] += part
-
-    total[0 : 6 * ROWS] = total[0 : 6 * ROWS] + total[6 * ROWS : 12 * ROWS]
+        values = [forces[3 * q : 3 * q + 3] + curves[3 * q : 3 * q + 3] for q in range(3)]
+        spread_out(values, k, hot_row, stage6, spread)
+
+    sweep(build, hot_lane, (spread6a, spread6b), total6)
     mass = inertia_of(whole)
     inverse = []
     for c in range(3):
         x = chunks(pos, c)
         bent = chain(x, whole[RIM + c : RIM + c + 1, :],
                      whole[(GROUPS - 1) * PACKED + RIM + c : (GROUPS - 1) * PACKED + RIM + c + 1, :])
-        felt, curve = chunks(total, c), chunks(total, 3 + c)
+        felt, curve = chunks(total6, c), chunks(total6, 3 + c)
         diag = [mass[k] + curve[k] + 2.0 * STIFF for k in range(VERT_CHUNKS)]
         inv = [1.0 / diag[k] for k in range(VERT_CHUNKS)]
         grad = [mass[k] * (x[k] - lane_rows(whole, TGT + 3 * k + c)) + bent[k] + felt[k]
@@ -227,7 +251,7 @@
         put(diagonal, c, diag)
         put(first, c, [-grad[k] * inv[k] for k in range(VERT_CHUNKS)])
         inverse.append(inv)
-    w = apply_local(whole, factors, first, stage, total)
+    w = apply_local(whole, factors, (hot_lane, hot_row), first, stage, (spread_a, spread_b), total)
     up[...] = jnp.zeros_like(up)
     down[...] = jnp.zeros_like(down)
     for c in range(3):
@@ -239,8 +263,9 @@
             down[3 * i + c : 3 * i + c + 1, :] = what[0][0:1, :]
 
 
-def krylov_kernel(whole, factors, first, image, diagonal, above, below,
-                  second, third, last_image, sums, stage, total):
+def krylov_kernel(whole, factors, hot_lane, hot_row, first, image, diagonal, above, below,
+                  second, third, last_image, sums, stage, spread_a, spread_b, total):
+    hots, spreads = (hot_lane, hot_row), (spread_a, spread_b)
     lane = iota((GROUPS, LANES), 1)
     sub = iota((GROUPS, LANES), 0)
     head = (lane == 0) & (sub == 0)
@@ -262,11 +287,11 @@
         mine_high = pltpu.roll(spread(v0[1][GROUPS - 1 : GROUPS, :]), 1, 1)[0:1, :]
         befores.append(above[3 + c : 4 + c, :] - STIFF * mine_low * above[6 + c : 7 + c, :])
         afters.append(below[3 + c : 4 + c, :] - STIFF * mine_high * below[6 + c : 7 + c, :])
-    w = apply_local(whole, factors, second, stage, total, befores, afters)
+    w = apply_local(whole, factors, hots, second, stage, spreads, total, befores, afters)
     for c in range(3):
         diag, v1 = chunks(diagonal, c), chunks(second, c)
         put(third, c, [w[c][k] / diag[k] - v1[k] for k in range(VERT_CHUNKS)])
-    w = apply_local(whole, factors, third, stage, total)
+    w = apply_local(whole, factors, hots, third, stage, spreads, total)
     moment = [0.0] * 6
     ends = []
     for c in range(3):
@@ -348,39 +373,45 @@
 
 def per_device(positions, target, inertia, incidence, rest_inverse, counts, w_in, w_hid1, w_hid2, w_out):
     patches = lax.axis_size("patch")
-    params = pltpu.CompilerParams(vmem_limit_bytes=48 * 1024 * 1024)
+    params = pltpu.CompilerParams(vmem_limit_bytes=16 * 1024 * 1024)
     swaps = []
     for p in range(patches - 1):
         left, right = p * GROUPS + GROUPS - 1, (p + 1) * GROUPS
         swaps += [(left, right), (right, left)]
     rim = lax.ppermute(positions, ("patch", "elem"), swaps)
-    packed = pl.pallas_call(
-        pack_kernel, out_shape=shape(GROUPS, PACKED, LANES),
-        in_specs=vmem(5) + [pl.BlockSpec(memory_space=pltpu.SMEM)] + vmem(1), out_specs=vmem(1)[0],
+    packed, weights = pl.pallas_call(
+        pack_kernel, out_shape=[shape(GROUPS, PACKED, LANES), jax.ShapeDtypeStruct((WEIGHTS, LANES), BF16)],
+        in_specs=vmem(5) + [pl.BlockSpec(memory_space=pltpu.SMEM)] + vmem(5), out_specs=vmem(2),
         name="pack",
-    )(positions, target, inertia, incidence, rest_inverse, counts, rim)
+    )(positions, target, inertia, incidence, rest_inverse, counts, w_in.T, w_hid1, w_hid2, w_out, rim)
     whole = lax.all_to_all(packed, "elem", 0, 0, tiled=True).reshape(GROUPS * PACKED, LANES)
     wide = 3 * ROWS
-    factors, first, image, diagonal, up, down = pl.pallas_call(
+    width = GROUPS * LANES
+
+    def scatter_scratch(comps):
+        spread = pltpu.VMEM((2 * comps * ROWS, 3 * width), BF16)
+        return [pltpu.VMEM((3, 2 * comps * GROUPS, LANES), F32), spread, spread,
+                pltpu.VMEM((2 * comps * ROWS, LANES), F32)]
+
+    factors, hot_lane, hot_row, first, image, diagonal, up, down = pl.pallas_call(
         setup_kernel,
-        out_shape=[shape(81 * TRI_ROWS, LANES), shape(wide, LANES), shape(wide, LANES), shape(wide, LANES),
-                   shape(16, LANES), shape(16, LANES)],
-        in_specs=vmem(5), out_specs=vmem(6),
+        out_shape=[shape(81 * TRI_ROWS, LANES), jax.ShapeDtypeStruct((TRI_CHUNKS, LANES, 3 * width), BF16),
+                   jax.ShapeDtypeStruct((TRI_CHUNKS, ROWS, 3 * width), BF16),
+                   shape(wide, LANES), shape(wide, LANES), shape(wide, LANES), shape(16, LANES), shape(16, LANES)],
+        in_specs=vmem(2), out_specs=vmem(8),
         scratch_shapes=[pltpu.VMEM((wide, LANES), F32), pltpu.VMEM((GROUPS * 16, LANES), F32),
-                        pltpu.VMEM((LANES, 16), F32), pltpu.VMEM((96, LANES), F32),
-                        pltpu.VMEM((96 * GROUPS, LANES), F32), pltpu.VMEM((14 * GROUPS, LANES), F32),
-                        pltpu.VMEM((12 * ROWS, LANES), F32)],
+                        pltpu.VMEM((TRI_CHUNKS, 16, width), BF16), pltpu.VMEM((TRI_CHUNKS, 96, width), F32),
+                        pltpu.VMEM((96 * GROUPS, LANES), F32)] + scatter_scratch(6) + scatter_scratch(3),
         compiler_params=params, name="setup",
-    )(whole, w_in, w_hid1, w_hid2, w_out)
+    )(whole, weights)
     above = lax.ppermute(up, "patch", [(p, p + 1) for p in range(patches - 1)])
     below = lax.ppermute(down, "patch", [(p + 1, p) for p in range(patches - 1)])
     second, third, last_image, sums = pl.pallas_call(
         krylov_kernel,
         out_shape=[shape(wide, LANES), shape(wide, LANES), shape(wide, LANES), shape(patches, LANES)],
-        in_specs=vmem(7), out_specs=vmem(4),
-        scratch_shapes=[pltpu.VMEM((8 * GROUPS, LANES), F32), pltpu.VMEM((6 * ROWS, LANES), F32)],
+        in_specs=vmem(9), out_specs=vmem(4), scratch_shapes=scatter_scratch(3),
         compiler_params=params, name="krylov",
-    )(whole, factors, first, image, diagonal, above, below)
+    )(whole, factors, hot_lane, hot_row, first, image, diagonal, above, below)
     sums = lax.all_to_all(sums, "patch", 0, 0, tiled=True)
     return pl.pallas_call(
         finish_kernel, out_shape=[shape(*positions.shape)] * 2,

time: 105 us -> 99.5 us (0.948)
  blocking collectives: 40.8 us -> 54.7 us
  waiting for transfers between devices: 10.2 us -> 1.73 us
  starting transfers between devices: 21.6 us -> 17.1 us
  Pallas kernels: 26.6 us -> 22.8 us
  local copies, waits for them, and re-layouts: 3.65 us -> 1.48 us
    all_to_all x0 -> x1, blocking collectives: none -> 13.9 us  [per_device(): lax.all_to_all(packed, 'elem', 0, 0, tiled=True)]
    all_to_all x1 -> x0, waiting for transfers between devices: 8.52 us -> none  [per_device(): lax.all_to_all(packed, 'elem', 0, 0, tiled=True)]
    all_to_all x1 -> x0, starting transfers between devices: 4.59 us -> none  [per_device(): lax.all_to_all(packed, 'elem', 0, 0, tiled=True)]
    pallas_call x1, Pallas kernels: 9.73 us -> 7.52 us  [per_device(): pl.pallas_call(krylov_kernel, out_shape=[shape(wide, LANES), shape(wide,...]
    unnamed x9 -> x4, local copies, waits for them, and re-layouts: 3.65 us -> 1.48 us
    pallas_call x2, Pallas kernels: 16 us -> 14.5 us  [the longest x1 12.9 us: per_device(): pl.pallas_call(setup_kernel, out_shape=[shape(81 * TRI_ROWS, LANES), jax....]
  transfers between devices with their start and end apart: 4 -> 3, of which waited for: 3 -> 2; matrix products, arithmetic and copies ran while one was open for 1% -> 0% of each run, Pallas kernels for 0% -> 0%
where the time goes in v2:
time: 99.5 us; the launch traced here: 99.1 us
  blocking collectives  54.7 us (55%)
  Pallas kernels  22.8 us (23%)
  starting transfers between devices  17.1 us (17%)
  waiting for transfers between devices  1.73 us (2%)
  local copies, waits for them, and re-layouts  1.48 us (1%)
  between operations  1.32 us (1%)
    all_to_all x1, blocking collectives, per_device(): sums = lax.all_to_all(sums, 'patch', 0, 0, tiled=True)  40.8 us
    all_to_all x1, blocking collectives, per_device(): lax.all_to_all(packed, 'elem', 0, 0, tiled=True)  13.9 us
    pallas_call x1, Pallas kernels, per_device(): pl.pallas_call(setup_kernel, out_shape=[shape(81 * TRI_ROWS, LANES), jax....  12.9 us
    pallas_call x1, Pallas kernels, per_device(): pl.pallas_call(krylov_kernel, out_shape=[shape(wide, LANES), shape(wide,...  7.52 us
    ppermute x1, starting transfers between devices, per_device(): above = lax.ppermute(up, 'patch', [(p, p + 1) for p in range(patches - 1)])  6.5 us
    ppermute x1, starting transfers between devices, per_device(): rim = lax.ppermute(positions, ('patch', 'elem'), swaps)  6.49 us
    ppermute x1, starting transfers between devices, per_device(): lax.ppermute(down, 'patch', [(p + 1, p) for p in range(patches - 1)])  4.07 us
  transfers between devices with their start and end apart: 3, of which 2 were waited for; matrix products, arithmetic and copies ran while one was open for 0% of the time, Pallas kernels for 0%

profile of v2, /device:TPU:1, one launch (start us, length us, event | category | flops | bytes accessed | tf_op | source)
XLA Modules:
  0.0 99.1 jit_solution(16446117138563633462)
XLA Ops:
  0.6 6.5 %collective-permute-start = (f32[3,256]{1,0:T(4,128)}, f32[3,256]{1,0:T(4,128)S(1)}, u32[]{:S(2)}, u32[]{:S(2)}) collective-permute-start(f32[3,256]{1,0:T(4,128)} %pos.1), channel_id=1, source_target_pairs={{7,8},{8,7},{15,16},{16,15},{23,24},{24,23},{31,32},{32,31},{39,40... | collective-permute-start | bytes 9224 | tf_op jit(solution)/shard_map/ppermute | solution.py:381
  7.8 0.8 collective-permute-done.rim
  8.6 0.0 copy-start.1
  8.6 0.6 copy-done.1
  9.2 1.6 %pack.1 = (f32[8,64,128]{2,1,0:T(8,128)}, bf16[368,128]{1,0:T(8,128)(2,1)}) custom-call(f32[3,256]{1,0:T(4,128)} %pos.1, f32[3,256]{1,0:T(4,128)} %tgt.1, f32[1,256]{1,0:T(1,128)} %inertia.1, s32[3,768]{1,0:T(4,128)} %inc.1, f32[4,768]{1,0:T(4,128)} %rinv.1, s32[1]{0:T(128)S(6)} %copy.13.counts, bf16[6,128]{1,0:T(8,128)(2,1)} %bitcast.10, ...), custom_call_target="tpu_custom_call" | custom-call | tf_op jit(solution)/shard_map/pack/pallas_call | solution.py:382
  10.8 13.9 %all_to_all.16 = f32[8,64,128]{2,1,0:T(8,128)S(1)} all-to-all(f32[8,64,128]{2,1,0:T(8,128)} %get-tuple-element.16), channel_id=1, replica_groups=mesh['patch'=128,'elem'=8] {'elem'}, dimensions={0} | all-to-all | bytes 524288 | tf_op jit(solution)/shard_map/all_to_all | solution.py:387
  24.7 0.0 copy-start
  24.8 0.9 copy-done
  25.6 12.9 %setup.1 = (f32[3888,128]{1,0:T(8,128)S(1)}, bf16[6,128,3072]{2,1,0:T(8,128)(2,1)S(1)}, bf16[6,16,3072]{2,1,0:T(8,128)(2,1)S(1)}, f32[48,128]{1,0:T(8,128)S(1)},...) custom-call(f32[512,128]{1,0:T(8,128)S(1)} %bitcast.6, ...), custom_call_target="tpu_custom_call" | custom-call | tf_op jit(solution)/shard_map/setup/pallas_call | solution.py:396
  38.5 6.5 %collective-permute-start.1 = (f32[16,128]{1,0:T(8,128)S(1)}, f32[16,128]{1,0:T(8,128)S(1)}, u32[]{:S(2)}, u32[]{:S(2)}) collective-permute-start(f32[16,128]{1,0:T(8,128)S(1)} %get-tuple-element.24), channel_id=1, source_target_pairs={{0,8},{8,16},{16,24},{24,32},{32,40},{40,48},{48,56},{56,64},{64,7... | collective-permute-start | bytes 24584 | tf_op jit(solution)/shard_map/ppermute | solution.py:407
  45.0 4.1 %collective-permute-start.2 = (f32[16,128]{1,0:T(8,128)S(1)}, f32[16,128]{1,0:T(8,128)S(1)}, u32[]{:S(2)}, u32[]{:S(2)}) collective-permute-start(f32[16,128]{1,0:T(8,128)S(1)} %get-tuple-element.25), channel_id=1, source_target_pairs={{8,0},{16,8},{24,16},{32,24},{40,32},{48,40},{56,48},{64,56},{72,6... | collective-permute-start | bytes 24584 | tf_op jit(solution)/shard_map/ppermute | solution.py:408
  49.1 0.0 collective-permute-done.1.above
  49.1 0.9 collective-permute-done.2.below
  50.0 7.5 %krylov.1 = (f32[48,128]{1,0:T(8,128)S(1)}, f32[48,128]{1,0:T(8,128)S(1)}, f32[48,128]{1,0:T(8,128)S(1)}, f32[128,128]{1,0:T(8,128)S(1)}) custom-call(f32[512,128]{1,0:T(8,128)S(1)} %bitcast.7, f32[3888,128]{1,0:T(8,128)S(1)} %get-tuple-element.18.factors, bf16[6,128,3072]{2,1,0:T(8,128)(2,1)S(1)} %get-tuple-element.19.hot_lane, ...), custom_call_target="tpu_custom_call" | custom-call | tf_op jit(solution)/shard_map/krylov/pallas_call | solution.py:409
  57.5 40.8 %all_to_all.17 = f32[128,1,128]{2,1,0:T(1,128)S(1)} all-to-all(f32[128,1,128]{2,1,0:T(1,128)S(1)} %bitcast.9), channel_id=1, replica_groups=mesh['patch'=128,'elem'=8] {'patch'}, dimensions={0} | all-to-all | bytes 131072 | tf_op jit(solution)/shard_map/all_to_all | solution.py:415
  98.3 0.8 finish.1
Async XLA Ops:
  0.6 8.0 %collective-permute-start = (f32[3,256]{1,0:T(4,128)}, f32[3,256]{1,0:T(4,128)S(1)}, u32[]{:S(2)}, u32[]{:S(2)}) collective-permute-start(f32[3,256]{1,0:T(4,128)} %pos.1), channel_id=1, source_target_pairs={{7,8},{8,7},{15,16},{16,15},{23,24},{24,23},{31,32},{32,31},{39,40... | collective-permute-start | bytes 9224 | tf_op jit(solution)/shard_map/ppermute | solution.py:381
  8.6 0.6 copy-start.1
  24.7 0.9 copy-start
  38.5 10.6 %collective-permute-start.1 = (f32[16,128]{1,0:T(8,128)S(1)}, f32[16,128]{1,0:T(8,128)S(1)}, u32[]{:S(2)}, u32[]{:S(2)}) collective-permute-start(f32[16,128]{1,0:T(8,128)S(1)} %get-tuple-element.24), channel_id=1, source_target_pairs={{0,8},{8,16},{16,24},{24,32},{32,40},{40,48},{48,56},{56,64},{64,7... | collective-permute-start | bytes 24584 | tf_op jit(solution)/shard_map/ppermute | solution.py:407
  45.0 5.0 %collective-permute-start.2 = (f32[16,128]{1,0:T(8,128)S(1)}, f32[16,128]{1,0:T(8,128)S(1)}, u32[]{:S(2)}, u32[]{:S(2)}) collective-permute-start(f32[16,128]{1,0:T(8,128)S(1)} %get-tuple-element.25), channel_id=1, source_target_pairs={{8,0},{16,8},{24,16},{32,24},{40,32},{48,40},{56,48},{64,56},{72,6... | collective-permute-start | bytes 24584 | tf_op jit(solution)/shard_map/ppermute | solution.py:408

commit v3 on v2

--- a/solution.py
+++ b/solution.py
@@ -19,6 +19,8 @@
 POS, TGT, INERTIA, COUNT, INC, RINV, RIM, PACKED = 0, 6, 12, 14, 16, 34, 58, 64
 
 HID1, HID2, LAST, WEIGHTS = 16, 144, 272, 368
+
+SHARED = 16
 
 F32 = jnp.float32
 BF16 = jnp.bfloat16
@@ -114,18 +116,12 @@
 
 def sweep(build, hot_lane, spreads, total):
     total[...] = jnp.zeros_like(total)
-    spreads[1][...] = jnp.zeros_like(spreads[1])
-
-    @pl.loop(0, TRI_CHUNKS // 2)
-    def _(i):
-        for half in range(2):
-            k = 2 * i + half
-            part = collect(spreads[1 - half], jnp.maximum(k - 1, 0), hot_lane)
-            build(k, spreads[half])
-            total[...] += part
-
+    for k in range(TRI_CHUNKS):
+        if k > 0:
+            total[...] += collect(spreads[(k - 1) % 2], k - 1, hot_lane)
+        build(k, spreads[k % 2], k % 2)
     half = total.shape[0] // 2
-    whole = total[...] + collect(spreads[1], TRI_CHUNKS - 1, hot_lane)
+    whole = total[...] + collect(spreads[(TRI_CHUNKS - 1) % 2], TRI_CHUNKS - 1, hot_lane)
     total[0:half] = whole[:half] + whole[half:]
 
 
@@ -158,9 +154,16 @@
 
 
 def elements(whole, factors, hot_lane, hot_row, field, stage, spreads, total):
-    def build(k, spread):
-        found = gather(field, [corner_of(whole, k, q) for q in range(3)])
+    def find(k):
+        return gather(field, [corner_of(whole, k, q) for q in range(3)])
+
+    ahead = [find(0)]
+
+    def build(k, spread, turn):
+        found = ahead.pop()
         u = found[0] + found[1] + found[2]
+        if k + 1 < TRI_CHUNKS:
+            ahead.append(find(k + 1))
 
         def factor(j, m):
             return factors[pl.ds(pl.multiple_of((9 * j + m) * TRI_ROWS + k * GROUPS, GROUPS), GROUPS), :]
@@ -168,7 +171,7 @@
         inner = [sum(factor(j, m) * u[j] for j in range(9)) * (1.0 / 9.0) for m in range(9)]
         shift = REG * valid_of(whole, k)
         out = [sum(factor(j, m) * inner[m] for m in range(9)) + shift * u[j] for j in range(9)]
-        spread_out([out[0:3], out[3:6], out[6:9]], k, hot_row, stage, spread)
+        spread_out([out[0:3], out[3:6], out[6:9]], k, hot_row, stage.at[turn], spread)
 
     sweep(build, hot_lane, spreads, total)
 
@@ -200,7 +203,7 @@
     def _(k):
         places = [corner_of(whole, k, q) for q in range(3)]
         for q, (row, lane) in enumerate(places):
-            one_hot(row, lane, q, k, hot_lane, hot_row, stage.at[q])
+            one_hot(row, lane, q, k, hot_lane, hot_row, stage.at[0, q])
         x0, x1, x2 = gather(pos, places)
         a, b, c_, d = [lane_rows(whole, RINV + 4 * k + i) for i in range(4)]
         for c in range(3):
@@ -218,7 +221,7 @@
     for k in range(TRI_CHUNKS):
         outputs[k] = o[:, k * GROUPS * LANES : (k + 1) * GROUPS * LANES]
 
-    def build(k, spread):
+    def build(k, spread, turn):
         for e in range(GROUPS):
             for g in range(12):
                 raw[pl.ds(g * 64 + e, 8, stride=8), :] = outputs[k, 8 * g : 8 * g + 8, e * LANES : (e + 1) * LANES]
@@ -234,7 +237,7 @@
                 curve += g * g
             curves.append(curve * (1.0 / 9.0) + REG * valid)
         values = [forces[3 * q : 3 * q + 3] + curves[3 * q : 3 * q + 3] for q in range(3)]
-        spread_out(values, k, hot_row, stage6, spread)
+        spread_out(values, k, hot_row, stage6.at[turn], spread)
 
     sweep(build, hot_lane, (spread6a, spread6b), total6)
     mass = inertia_of(whole)
@@ -308,7 +311,7 @@
     for i, part in enumerate(moment + [x[0] for x in ends] + [x[1] for x in ends]):
         value = jnp.sum(jnp.sum(part, axis=0, keepdims=True), axis=1, keepdims=True)
         line = jnp.where(iota((1, LANES), 1) == i, value, line)
-    sums[...] = jnp.broadcast_to(line, sums.shape)
+    sums[...] = jnp.broadcast_to(line[:, 0:SHARED], sums.shape)
 
 
 def finish_kernel(sums, first, second, third, last_image, diagonal, field, residual):
@@ -320,7 +323,7 @@
     totals = jnp.sum(every, axis=0, keepdims=True)
 
     def pick(row, i):
-        return jnp.sum(jnp.where(iota((1, LANES), 1) == i, row, 0.0), axis=1, keepdims=True)
+        return row[:, i : i + 1]
 
     after = pltpu.roll(pltpu.roll(every, patches - 1, 0), 3, 1)
     coupled = jnp.where((lane >= 9) & (lane < 12) & (sub < patches - 1), every * after, 0.0)
@@ -390,7 +393,7 @@
 
     def scatter_scratch(comps):
         spread = pltpu.VMEM((2 * comps * ROWS, 3 * width), BF16)
-        return [pltpu.VMEM((3, 2 * comps * GROUPS, LANES), F32), spread, spread,
+        return [pltpu.VMEM((2, 3, 2 * comps * GROUPS, LANES), F32), spread, spread,
                 pltpu.VMEM((2 * comps * ROWS, LANES), F32)]
 
     factors, hot_lane, hot_row, first, image, diagonal, up, down = pl.pallas_call(
@@ -408,7 +411,7 @@
     below = lax.ppermute(down, "patch", [(p + 1, p) for p in range(patches - 1)])
     second, third, last_image, sums = pl.pallas_call(
         krylov_kernel,
-        out_shape=[shape(wide, LANES), shape(wide, LANES), shape(wide, LANES), shape(patches, LANES)],
+        out_shape=[shape(wide, LANES), shape(wide, LANES), shape(wide, LANES), shape(patches, SHARED)],
         in_specs=vmem(9), out_specs=vmem(4), scratch_shapes=scatter_scratch(3),
         compiler_params=params, name="krylov",
     )(whole, factors, hot_lane, hot_row, first, image, diagonal, above, below)

time: 99.5 us -> 97.9 us (0.984)
  Pallas kernels: 22.8 us -> 21.2 us
where the time goes in v3:
time: 97.9 us; the launch traced here: 97.5 us
  blocking collectives  54.7 us (56%)
  Pallas kernels  21.2 us (22%)
  starting transfers between devices  17.2 us (18%)
  waiting for transfers between devices  1.55 us (2%)
  local copies, waits for them, and re-layouts  1.48 us (2%)
  between operations  1.32 us (1%)
    all_to_all x1, blocking collectives, per_device(): sums = lax.all_to_all(sums, 'patch', 0, 0, tiled=True)  40.8 us
    all_to_all x1, blocking collectives, per_device(): lax.all_to_all(packed, 'elem', 0, 0, tiled=True)  13.9 us
    pallas_call x1, Pallas kernels, per_device(): pl.pallas_call(setup_kernel, out_shape=[shape(81 * TRI_ROWS, LANES), jax....  11.9 us
    pallas_call x1, Pallas kernels, per_device(): pl.pallas_call(krylov_kernel, out_shape=[shape(wide, LANES), shape(wide,...  6.6 us
    ppermute x1, starting transfers between devices, per_device(): above = lax.ppermute(up, 'patch', [(p, p + 1) for p in range(patches - 1)])  6.5 us
    ppermute x1, starting transfers between devices, per_device(): rim = lax.ppermute(positions, ('patch', 'elem'), swaps)  6.49 us
    ppermute x1, starting transfers between devices, per_device(): lax.ppermute(down, 'patch', [(p + 1, p) for p in range(patches - 1)])  4.25 us
  transfers between devices with their start and end apart: 3, of which 2 were waited for; matrix products, arithmetic and copies ran while one was open for 0% of the time, Pallas kernels for 0%

profile of v3, /device:TPU:1, one launch (start us, length us, event | category | flops | bytes accessed | tf_op | source)
XLA Modules:
  0.0 97.5 jit_solution(5392501015618481260)
XLA Ops:
  0.6 6.5 %collective-permute-start = (f32[3,256]{1,0:T(4,128)}, f32[3,256]{1,0:T(4,128)S(1)}, u32[]{:S(2)}, u32[]{:S(2)}) collective-permute-start(f32[3,256]{1,0:T(4,128)} %pos.1), channel_id=1, source_target_pairs={{7,8},{8,7},{15,16},{16,15},{23,24},{24,23},{31,32},{32,31},{39,40... | collective-permute-start | bytes 9224 | tf_op jit(solution)/shard_map/ppermute | solution.py:384
  7.8 0.8 collective-permute-done.rim
  8.6 0.0 copy-start.1
  8.6 0.6 copy-done.1
  9.2 1.6 %pack.1 = (f32[8,64,128]{2,1,0:T(8,128)}, bf16[368,128]{1,0:T(8,128)(2,1)}) custom-call(f32[3,256]{1,0:T(4,128)} %pos.1, f32[3,256]{1,0:T(4,128)} %tgt.1, f32[1,256]{1,0:T(1,128)} %inertia.1, s32[3,768]{1,0:T(4,128)} %inc.1, f32[4,768]{1,0:T(4,128)} %rinv.1, s32[1]{0:T(128)S(6)} %copy.13.counts, bf16[6,128]{1,0:T(8,128)(2,1)} %bitcast.10, ...), custom_call_target="tpu_custom_call" | custom-call | tf_op jit(solution)/shard_map/pack/pallas_call | solution.py:385
  10.8 13.9 %all_to_all.16 = f32[8,64,128]{2,1,0:T(8,128)S(1)} all-to-all(f32[8,64,128]{2,1,0:T(8,128)} %get-tuple-element.16), channel_id=1, replica_groups=mesh['patch'=128,'elem'=8] {'elem'}, dimensions={0} | all-to-all | bytes 524288 | tf_op jit(solution)/shard_map/all_to_all | solution.py:390
  24.7 0.0 copy-start
  24.8 0.9 copy-done
  25.6 11.9 %setup.1 = (f32[3888,128]{1,0:T(8,128)S(1)}, bf16[6,128,3072]{2,1,0:T(8,128)(2,1)S(1)}, bf16[6,16,3072]{2,1,0:T(8,128)(2,1)S(1)}, f32[48,128]{1,0:T(8,128)S(1)},...) custom-call(f32[512,128]{1,0:T(8,128)S(1)} %bitcast.6, ...), custom_call_target="tpu_custom_call" | custom-call | tf_op jit(solution)/shard_map/setup/pallas_call | solution.py:399
  37.6 6.5 %collective-permute-start.1 = (f32[16,128]{1,0:T(8,128)S(1)}, f32[16,128]{1,0:T(8,128)S(1)}, u32[]{:S(2)}, u32[]{:S(2)}) collective-permute-start(f32[16,128]{1,0:T(8,128)S(1)} %get-tuple-element.24), channel_id=1, source_target_pairs={{0,8},{8,16},{16,24},{24,32},{32,40},{40,48},{48,56},{56,64},{64,7... | collective-permute-start | bytes 24584 | tf_op jit(solution)/shard_map/ppermute | solution.py:410
  44.1 4.2 %collective-permute-start.2 = (f32[16,128]{1,0:T(8,128)S(1)}, f32[16,128]{1,0:T(8,128)S(1)}, u32[]{:S(2)}, u32[]{:S(2)}) collective-permute-start(f32[16,128]{1,0:T(8,128)S(1)} %get-tuple-element.25), channel_id=1, source_target_pairs={{8,0},{16,8},{24,16},{32,24},{40,32},{48,40},{56,48},{64,56},{72,6... | collective-permute-start | bytes 24584 | tf_op jit(solution)/shard_map/ppermute | solution.py:411
  48.3 0.0 collective-permute-done.1.above
  48.3 0.7 collective-permute-done.2.below
  49.0 6.6 %krylov.1 = (f32[48,128]{1,0:T(8,128)S(1)}, f32[48,128]{1,0:T(8,128)S(1)}, f32[48,128]{1,0:T(8,128)S(1)}, f32[128,16]{1,0:T(8,128)S(1)}) custom-call(f32[512,128]{1,0:T(8,128)S(1)} %bitcast.7, f32[3888,128]{1,0:T(8,128)S(1)} %get-tuple-element.18.factors, bf16[6,128,3072]{2,1,0:T(8,128)(2,1)S(1)} %get-tuple-element.19.hot_lane, ...), custom_call_target="tpu_custom_call" | custom-call | tf_op jit(solution)/shard_map/krylov/pallas_call | solution.py:412
  55.6 40.8 %all_to_all.17 = f32[128,1,16]{2,1,0:T(1,128)S(1)} all-to-all(f32[128,1,16]{2,1,0:T(1,128)S(1)} %bitcast.9), channel_id=1, replica_groups=mesh['patch'=128,'elem'=8] {'patch'}, dimensions={0} | all-to-all | bytes 16384 | tf_op jit(solution)/shard_map/all_to_all | solution.py:418
  96.4 1.1 %finish.1 = (f32[3,256]{1,0:T(4,128)}, f32[3,256]{1,0:T(4,128)}) custom-call(f32[128,16]{1,0:T(8,128)S(1)} %bitcast.8, f32[48,128]{1,0:T(8,128)S(1)} %get-tuple-element.21.first, f32[48,128]{1,0:T(8,128)S(1)} %get-tuple-element.27.second, f32[48,128]{1,0:T(8,128)S(1)} %get-tuple-element.28.third, f32[48,128]{1,0:T(8,128)S(1)} %get-tuple-element.29.last_image, ...), custom_call_target="tpu_custom_call" | custom-call | tf_op jit(solution)/shard_map/finish/pallas_call | solution.py:419
Async XLA Ops:
  0.6 8.0 %collective-permute-start = (f32[3,256]{1,0:T(4,128)}, f32[3,256]{1,0:T(4,128)S(1)}, u32[]{:S(2)}, u32[]{:S(2)}) collective-permute-start(f32[3,256]{1,0:T(4,128)} %pos.1), channel_id=1, source_target_pairs={{7,8},{8,7},{15,16},{16,15},{23,24},{24,23},{31,32},{32,31},{39,40... | collective-permute-start | bytes 9224 | tf_op jit(solution)/shard_map/ppermute | solution.py:384
  8.6 0.6 copy-start.1
  24.7 0.9 copy-start
  37.6 10.8 %collective-permute-start.1 = (f32[16,128]{1,0:T(8,128)S(1)}, f32[16,128]{1,0:T(8,128)S(1)}, u32[]{:S(2)}, u32[]{:S(2)}) collective-permute-start(f32[16,128]{1,0:T(8,128)S(1)} %get-tuple-element.24), channel_id=1, source_target_pairs={{0,8},{8,16},{16,24},{24,32},{32,40},{40,48},{48,56},{56,64},{64,7... | collective-permute-start | bytes 24584 | tf_op jit(solution)/shard_map/ppermute | solution.py:410
  44.1 5.0 %collective-permute-start.2 = (f32[16,128]{1,0:T(8,128)S(1)}, f32[16,128]{1,0:T(8,128)S(1)}, u32[]{:S(2)}, u32[]{:S(2)}) collective-permute-start(f32[16,128]{1,0:T(8,128)S(1)} %get-tuple-element.25), channel_id=1, source_target_pairs={{8,0},{16,8},{24,16},{32,24},{40,32},{48,40},{56,48},{64,56},{72,6... | collective-permute-start | bytes 24584 | tf_op jit(solution)/shard_map/ppermute | solution.py:411

commit v4 on v3

--- a/solution.py
+++ b/solution.py
@@ -16,10 +16,11 @@
 ROWS = VERT_CHUNKS * GROUPS
 TRI_ROWS = TRI_CHUNKS * GROUPS
 
-POS, TGT, INERTIA, COUNT, INC, RINV, RIM, PACKED = 0, 6, 12, 14, 16, 34, 58, 64
+POS, TGT, INERTIA, INC, RINV, RIM, COUNT, PACKED = 0, 6, 12, 14, 32, 56, 59, 64
 
 HID1, HID2, LAST, WEIGHTS = 16, 144, 272, 368
 
+QUANTA = 2.0**20 - 1.0
 SHARED = 16
 
 F32 = jnp.float32
@@ -34,8 +35,7 @@
     return lax.broadcasted_iota(jnp.int32, shape, axis)
 
 
-def pack_kernel(pos, tgt, inertia, inc, rinv, counts, w_in, w_hid1, w_hid2, w_out, rim, out, weights):
-    first = lax.axis_index("elem") == 0
+def pack_kernel(pos, tgt, inertia, inc, rinv, w_in, w_hid1, w_hid2, w_out, out, weights):
     weights[0:16] = jnp.concatenate([w_in[...].astype(F32), jnp.zeros((10, LANES), F32)], axis=0).astype(BF16)
     weights[HID1:HID2] = w_hid1[...]
     weights[HID2:LAST] = w_hid2[...]
@@ -46,15 +46,22 @@
         out[0, POS + 3 * k : POS + 3 * k + 3] = pos[:, cut]
         out[0, TGT + 3 * k : TGT + 3 * k + 3] = tgt[:, cut]
         out[0, INERTIA + k : INERTIA + k + 1] = inertia[:, cut]
-    out[0, COUNT : COUNT + 1] = jnp.full((1, LANES), counts[0], jnp.int32).astype(F32)
     for k in range(TRI_CHUNKS):
         cut = slice(k * LANES, (k + 1) * LANES)
         out[0, INC + 3 * k : INC + 3 * k + 3] = inc[:, cut].astype(F32)
         out[0, RINV + 4 * k : RINV + 4 * k + 4] = rinv[:, cut]
-    out[0, RIM : RIM + 3] = jnp.where(first, rim[:, LANES:], rim[:, :LANES])
     block = out[0]
     for e in range(1, GROUPS):
         out[e] = block
+
+
+def rim_kernel(packed, rim, counts, out):
+    del packed
+    first = lax.axis_index("elem") == 0
+    ends = jnp.where(first, rim[:, :LANES], rim[:, LANES:])
+    count = jnp.full((1, LANES), counts[0], jnp.int32).astype(F32)
+    tile = jnp.concatenate([ends, count, jnp.zeros((PACKED - COUNT - 1, LANES), F32)], axis=0)
+    out[...] = jnp.broadcast_to(tile[None], out.shape)
 
 
 def lane_rows(ref, row):
@@ -93,6 +100,31 @@
                 value = jnp.take_along_axis(line, lane, axis=1, mode="promise_in_bounds")
                 found[q][c] = jnp.where(here[q], value, found[q][c])
     return found
+
+
+def quantized(field, words):
+    top = jnp.max(jnp.max(jnp.abs(field[...]), axis=0, keepdims=True), axis=1, keepdims=True)
+    step = jnp.maximum(top, 1e-32) / QUANTA
+    x, y, z = [jnp.round(field[c * ROWS : (c + 1) * ROWS] * (1.0 / step)).astype(jnp.int32) for c in range(3)]
+    words[0:ROWS] = (x << 11) | ((z >> 10) & 2047)
+    words[ROWS : 2 * ROWS] = (y << 11) | (z & 1023)
+    return step
+
+
+def gather_words(words, step, places):
+    found = [[jnp.zeros((GROUPS, LANES), jnp.int32)] * 2 for _ in places]
+    for h in range(ROWS):
+        here = [row == h for row, _ in places]
+        for w in range(2):
+            line = jnp.broadcast_to(words[w * ROWS + h : w * ROWS + h + 1, :], (GROUPS, LANES))
+            for q, (_, lane) in enumerate(places):
+                value = jnp.take_along_axis(line, lane, axis=1, mode="promise_in_bounds")
+                found[q][w] = jnp.where(here[q], value, found[q][w])
+    out = []
+    for one, two in found:
+        parts = (one >> 11, two >> 11, (((one << 21) >> 21) << 10) | (two & 1023))
+        out.append([part.astype(F32) * step for part in parts])
+    return out
 
 
 def spread_out(values, k, hot_row, stage, spread):
@@ -153,9 +185,11 @@
     ref[at + GROUPS : at + ROWS, :] = pair[1]
 
 
-def elements(whole, factors, hot_lane, hot_row, field, stage, spreads, total):
+def elements(whole, factors, hot_lane, hot_row, field, words, stage, spreads, total):
+    step = quantized(field, words)
+
     def find(k):
-        return gather(field, [corner_of(whole, k, q) for q in range(3)])
+        return gather_words(words, step, [corner_of(whole, k, q) for q in range(3)])
 
     ahead = [find(0)]
 
@@ -180,8 +214,8 @@
     return [lane_rows(whole, INERTIA + k) for k in range(VERT_CHUNKS)]
 
 
-def apply_local(whole, factors, hots, field, stage, spreads, total, befores=None, afters=None):
-    elements(whole, factors, *hots, field, stage, spreads, total)
+def apply_local(whole, factors, hots, field, words, stage, spreads, total, befores=None, afters=None):
+    elements(whole, factors, *hots, field, words, stage, spreads, total)
     mass = inertia_of(whole)
     out = []
     for c in range(3):
@@ -194,23 +228,23 @@
 
 def setup_kernel(whole, weights, factors, hot_lane, hot_row, first, image, diagonal, up, down,
                  pos, feats, inputs, outputs, raw, stage6, spread6a, spread6b, total6,
-                 stage, spread_a, spread_b, total):
+                 words, stage, spread_a, spread_b, total):
     for c in range(3):
         put(pos, c, [lane_rows(whole, POS + 3 * k + c) for k in range(VERT_CHUNKS)])
     feats[...] = jnp.zeros_like(feats)
 
-    @pl.loop(0, TRI_CHUNKS)
-    def _(k):
+    for k in range(TRI_CHUNKS):
+        feat = feats.at[k % 2]
         places = [corner_of(whole, k, q) for q in range(3)]
         for q, (row, lane) in enumerate(places):
-            one_hot(row, lane, q, k, hot_lane, hot_row, stage.at[0, q])
+            one_hot(row, lane, q, k, hot_lane, hot_row, stage.at[k % 2, q])
         x0, x1, x2 = gather(pos, places)
         a, b, c_, d = [lane_rows(whole, RINV + 4 * k + i) for i in range(4)]
         for c in range(3):
             one, two = x1[c] - x0[c], x2[c] - x0[c]
-            feats[pl.ds(c, GROUPS, stride=16), :] = one * a + two * c_
-            feats[pl.ds(3 + c, GROUPS, stride=16), :] = one * b + two * d
-        inputs[k] = jnp.concatenate([feats[16 * e : 16 * e + 16, :] for e in range(GROUPS)], axis=1).astype(BF16)
+            feat[pl.ds(c, GROUPS, stride=16), :] = one * a + two * c_
+            feat[pl.ds(3 + c, GROUPS, stride=16), :] = one * b + two * d
+        inputs[k] = jnp.concatenate([feat[16 * e : 16 * e + 16, :] for e in range(GROUPS)], axis=1).astype(BF16)
 
     x = jnp.concatenate([inputs[k] for k in range(TRI_CHUNKS)], axis=1)
     h = lax.dot_general(weights[0:HID1], x, (((0,), (0,)), ((), ())), preferred_element_type=F32)
@@ -244,8 +278,8 @@
     inverse = []
     for c in range(3):
         x = chunks(pos, c)
-        bent = chain(x, whole[RIM + c : RIM + c + 1, :],
-                     whole[(GROUPS - 1) * PACKED + RIM + c : (GROUPS - 1) * PACKED + RIM + c + 1, :])
+        bent = chain(x, whole[(GROUPS - 1) * PACKED + RIM + c : (GROUPS - 1) * PACKED + RIM + c + 1, :],
+                     whole[RIM + c : RIM + c + 1, :])
         felt, curve = chunks(total6, c), chunks(total6, 3 + c)
         diag = [mass[k] + curve[k] + 2.0 * STIFF for k in range(VERT_CHUNKS)]
         inv = [1.0 / diag[k] for k in range(VERT_CHUNKS)]
@@ -254,7 +288,7 @@
         put(diagonal, c, diag)
         put(first, c, [-grad[k] * inv[k] for k in range(VERT_CHUNKS)])
         inverse.append(inv)
-    w = apply_local(whole, factors, (hot_lane, hot_row), first, stage, (spread_a, spread_b), total)
+    w = apply_local(whole, factors, (hot_lane, hot_row), first, words, stage, (spread_a, spread_b), total)
     up[...] = jnp.zeros_like(up)
     down[...] = jnp.zeros_like(down)
     for c in range(3):
@@ -267,7 +301,7 @@
 
 
 def krylov_kernel(whole, factors, hot_lane, hot_row, first, image, diagonal, above, below,
-                  second, third, last_image, sums, stage, spread_a, spread_b, total):
+                  second, third, last_image, sums, words, stage, spread_a, spread_b, total):
     hots, spreads = (hot_lane, hot_row), (spread_a, spread_b)
     lane = iota((GROUPS, LANES), 1)
     sub = iota((GROUPS, LANES), 0)
@@ -290,11 +324,11 @@
         mine_high = pltpu.roll(spread(v0[1][GROUPS - 1 : GROUPS, :]), 1, 1)[0:1, :]
         befores.append(above[3 + c : 4 + c, :] - STIFF * mine_low * above[6 + c : 7 + c, :])
         afters.append(below[3 + c : 4 + c, :] - STIFF * mine_high * below[6 + c : 7 + c, :])
-    w = apply_local(whole, factors, hots, second, stage, spreads, total, befores, afters)
+    w = apply_local(whole, factors, hots, second, words, stage, spreads, total, befores, afters)
     for c in range(3):
         diag, v1 = chunks(diagonal, c), chunks(second, c)
         put(third, c, [w[c][k] / diag[k] - v1[k] for k in range(VERT_CHUNKS)])
-    w = apply_local(whole, factors, hots, third, stage, spreads, total)
+    w = apply_local(whole, factors, hots, third, words, stage, spreads, total)
     moment = [0.0] * 6
     ends = []
     for c in range(3):
@@ -377,19 +411,25 @@
 def per_device(positions, target, inertia, incidence, rest_inverse, counts, w_in, w_hid1, w_hid2, w_out):
     patches = lax.axis_size("patch")
     params = pltpu.CompilerParams(vmem_limit_bytes=16 * 1024 * 1024)
-    swaps = []
+    moves = []
     for p in range(patches - 1):
-        left, right = p * GROUPS + GROUPS - 1, (p + 1) * GROUPS
-        swaps += [(left, right), (right, left)]
-    rim = lax.ppermute(positions, ("patch", "elem"), swaps)
+        left, right = p * GROUPS, (p + 1) * GROUPS
+        moves += [(left + GROUPS - 1, right + GROUPS - 1), (right, left)]
+    rim = lax.ppermute(positions, ("patch", "elem"), moves)
     packed, weights = pl.pallas_call(
         pack_kernel, out_shape=[shape(GROUPS, PACKED, LANES), jax.ShapeDtypeStruct((WEIGHTS, LANES), BF16)],
-        in_specs=vmem(5) + [pl.BlockSpec(memory_space=pltpu.SMEM)] + vmem(5), out_specs=vmem(2),
-        name="pack",
-    )(positions, target, inertia, incidence, rest_inverse, counts, w_in.T, w_hid1, w_hid2, w_out, rim)
+        in_specs=vmem(9), out_specs=vmem(2), name="pack",
+    )(positions, target, inertia, incidence, rest_inverse, w_in.T, w_hid1, w_hid2, w_out)
+    packed = pl.pallas_call(
+        rim_kernel, grid=(1,), out_shape=shape(GROUPS, PACKED, LANES),
+        in_specs=[pl.BlockSpec(memory_space=pl.ANY)] + vmem(1) + [pl.BlockSpec(memory_space=pltpu.SMEM)],
+        out_specs=pl.BlockSpec((GROUPS, PACKED - RIM, LANES), lambda i: (0, RIM // (PACKED - RIM), 0)),
+        input_output_aliases={0: 0}, name="rim",
+    )(packed, rim, counts)
     whole = lax.all_to_all(packed, "elem", 0, 0, tiled=True).reshape(GROUPS * PACKED, LANES)
     wide = 3 * ROWS
     width = GROUPS * LANES
+    words = [pltpu.VMEM((2 * ROWS, LANES), jnp.int32)]
 
     def scatter_scratch(comps):
         spread = pltpu.VMEM((2 * comps * ROWS, 3 * width), BF16)
@@ -402,9 +442,9 @@
                    jax.ShapeDtypeStruct((TRI_CHUNKS, ROWS, 3 * width), BF16),
                    shape(wide, LANES), shape(wide, LANES), shape(wide, LANES), shape(16, LANES), shape(16, LANES)],
         in_specs=vmem(2), out_specs=vmem(8),
-        scratch_shapes=[pltpu.VMEM((wide, LANES), F32), pltpu.VMEM((GROUPS * 16, LANES), F32),
+        scratch_shapes=[pltpu.VMEM((wide, LANES), F32), pltpu.VMEM((2, GROUPS * 16, LANES), F32),
                         pltpu.VMEM((TRI_CHUNKS, 16, width), BF16), pltpu.VMEM((TRI_CHUNKS, 96, width), F32),
-                        pltpu.VMEM((96 * GROUPS, LANES), F32)] + scatter_scratch(6) + scatter_scratch(3),
+                        pltpu.VMEM((96 * GROUPS, LANES), F32)] + scatter_scratch(6) + words + scatter_scratch(3),
         compiler_params=params, name="setup",
     )(whole, weights)
     above = lax.ppermute(up, "patch", [(p, p + 1) for p in range(patches - 1)])
@@ -412,7 +452,7 @@
     second, third, last_image, sums = pl.pallas_call(
         krylov_kernel,
         out_shape=[shape(wide, LANES), shape(wide, LANES), shape(wide, LANES), shape(patches, SHARED)],
-        in_specs=vmem(9), out_specs=vmem(4), scratch_shapes=scatter_scratch(3),
+        in_specs=vmem(9), out_specs=vmem(4), scratch_shapes=words + scatter_scratch(3),
         compiler_params=params, name="krylov",
     )(whole, factors, hot_lane, hot_row, first, image, diagonal, above, below)
     sums = lax.all_to_all(sums, "patch", 0, 0, tiled=True)

time: 97.9 us -> 94.9 us (0.969)
  blocking collectives: 54.7 us -> 48.3 us
  starting transfers between devices: 17.2 us -> 20.6 us
    ppermute x1, starting transfers between devices: 6.49 us -> 16.1 us  [per_device(): rim = lax.ppermute(positions, ('patch', 'elem'), moves)]
    all_to_all x1, blocking collectives: 40.8 us -> 32.7 us  [per_device(): sums = lax.all_to_all(sums, 'patch', 0, 0, tiled=True)]
    ppermute x1, starting transfers between devices: 6.5 us -> 1.92 us  [per_device(): above = lax.ppermute(up, 'patch', [(p, p + 1) for p in range(patches - 1)])]
    ppermute x1, starting transfers between devices: 4.25 us -> 2.58 us  [per_device(): lax.ppermute(down, 'patch', [(p + 1, p) for p in range(patches - 1)])]
    ppermute x1, waiting for transfers between devices: 0.7 us -> 2.37 us  [per_device(): lax.ppermute(down, 'patch', [(p + 1, p) for p in range(patches - 1)])]
    all_to_all x1, blocking collectives: 13.9 us -> 15.6 us  [per_device(): lax.all_to_all(packed, 'elem', 0, 0, tiled=True)]
    pallas_call x0 -> x1, Pallas kernels: none -> 1.3 us  [per_device(): pl.pallas_call(rim_kernel, grid=(1,), out_shape=shape(GROUPS, PACKED, LAN...]
    pallas_call x1, Pallas kernels: 6.6 us -> 5.38 us  [per_device(): pl.pallas_call(krylov_kernel, out_shape=[shape(wide, LANES), shape(wide,...]
  transfers between devices with their start and end apart: 3 -> 3, of which waited for: 2 -> 1; matrix products, arithmetic and copies ran while one was open for 0% -> 0% of each run, Pallas kernels for 0% -> 2%
where the time goes in v4:
time: 94.9 us; the launch traced here: 94.4 us
  blocking collectives  48.3 us (51%)
  starting transfers between devices  20.6 us (22%)
  Pallas kernels  20.4 us (21%)
  waiting for transfers between devices  2.37 us (2%)
  local copies, waits for them, and re-layouts  1.48 us (2%)
  between operations  1.32 us (1%)
    all_to_all x1, blocking collectives, per_device(): sums = lax.all_to_all(sums, 'patch', 0, 0, tiled=True)  32.7 us
    ppermute x1, starting transfers between devices, per_device(): rim = lax.ppermute(positions, ('patch', 'elem'), moves)  16.1 us
    all_to_all x1, blocking collectives, per_device(): lax.all_to_all(packed, 'elem', 0, 0, tiled=True)  15.6 us
    pallas_call x1, Pallas kernels, per_device(): pl.pallas_call(setup_kernel, out_shape=[shape(81 * TRI_ROWS, LANES), jax....  11 us
    pallas_call x1, Pallas kernels, per_device(): pl.pallas_call(krylov_kernel, out_shape=[shape(wide, LANES), shape(wide,...  5.38 us
    ppermute x1, starting transfers between devices, per_device(): lax.ppermute(down, 'patch', [(p + 1, p) for p in range(patches - 1)])  2.58 us
    ppermute x1, waiting for transfers between devices, per_device(): lax.ppermute(down, 'patch', [(p + 1, p) for p in range(patches - 1)])  2.37 us
    ppermute x1, starting transfers between devices, per_device(): above = lax.ppermute(up, 'patch', [(p, p + 1) for p in range(patches - 1)])  1.92 us
  transfers between devices with their start and end apart: 3, of which 1 were waited for; matrix products, arithmetic and copies ran while one was open for 0% of the time, Pallas kernels for 2%

profile of v4, /device:TPU:1, one launch (start us, length us, event | category | flops | bytes accessed | tf_op | source)
XLA Modules:
  0.0 94.4 jit_solution(15694702122449510414)
XLA Ops:
  0.6 16.1 %collective-permute-start = (f32[3,256]{1,0:T(4,128)}, f32[3,256]{1,0:T(4,128)S(1)}, u32[]{:S(2)}, u32[]{:S(2)}) collective-permute-start(f32[3,256]{1,0:T(4,128)} %pos.1), channel_id=1, source_target_pairs={{7,15},{8,0},{15,23},{16,8},{23,31},{24,16},{31,39},{32,24},{39,47... | collective-permute-start | bytes 9224 | tf_op jit(solution)/shard_map/ppermute | solution.py:418
  17.3 1.6 %pack.1 = (f32[8,64,128]{2,1,0:T(8,128)}, bf16[368,128]{1,0:T(8,128)(2,1)}) custom-call(f32[3,256]{1,0:T(4,128)} %pos.1, f32[3,256]{1,0:T(4,128)} %tgt.1, f32[1,256]{1,0:T(1,128)} %inertia.1, s32[3,768]{1,0:T(4,128)} %inc.1, f32[4,768]{1,0:T(4,128)} %rinv.1, bf16[6,128]{1,0:T(8,128)(2,1)} %bitcast.10, bf16[128,128]{1,0:T(8,128)(2,1)} %w_hid1.1, ...), custom_call_target="tpu_custom_call" | custom-call | tf_op jit(solution)/shard_map/pack/pallas_call | solution.py:419
  19.0 0.0 collective-permute-done.rim
  19.0 0.0 copy-start.1
  19.0 0.6 copy-done.1
  19.6 1.3 %rim.1 = f32[8,64,128]{2,1,0:T(8,128)} custom-call(f32[8,64,128]{2,1,0:T(8,128)} %get-tuple-element.16.packed, f32[3,256]{1,0:T(4,128)} %copy-done.1, s32[1]{0:T(128)S(6)} %copy.15.counts), custom_call_target="tpu_custom_call", output_to_operand_aliasing={{}: (0, {})} | custom-call | tf_op jit(solution)/shard_map/rim/pallas_call | solution.py:423
  20.9 15.6 %all_to_all.16 = f32[8,64,128]{2,1,0:T(8,128)S(1)} all-to-all(f32[8,64,128]{2,1,0:T(8,128)} %rim.1), channel_id=1, replica_groups=mesh['patch'=128,'elem'=8] {'elem'}, dimensions={0} | all-to-all | bytes 524288 | tf_op jit(solution)/shard_map/all_to_all | solution.py:429
  36.4 0.0 copy-start
  36.4 0.9 copy-done
  37.3 11.0 %setup.1 = (f32[3888,128]{1,0:T(8,128)S(1)}, bf16[6,128,3072]{2,1,0:T(8,128)(2,1)S(1)}, bf16[6,16,3072]{2,1,0:T(8,128)(2,1)S(1)}, f32[48,128]{1,0:T(8,128)S(1)},...) custom-call(f32[512,128]{1,0:T(8,128)S(1)} %bitcast.6, ...), custom_call_target="tpu_custom_call" | custom-call | tf_op jit(solution)/shard_map/setup/pallas_call | solution.py:439
  48.4 1.9 %collective-permute-start.1 = (f32[16,128]{1,0:T(8,128)S(1)}, f32[16,128]{1,0:T(8,128)S(1)}, u32[]{:S(2)}, u32[]{:S(2)}) collective-permute-start(f32[16,128]{1,0:T(8,128)S(1)} %get-tuple-element.24), channel_id=1, source_target_pairs={{0,8},{8,16},{16,24},{24,32},{32,40},{40,48},{48,56},{56,64},{64,7... | collective-permute-start | bytes 24584 | tf_op jit(solution)/shard_map/ppermute | solution.py:450
  50.3 2.6 %collective-permute-start.2 = (f32[16,128]{1,0:T(8,128)S(1)}, f32[16,128]{1,0:T(8,128)S(1)}, u32[]{:S(2)}, u32[]{:S(2)}) collective-permute-start(f32[16,128]{1,0:T(8,128)S(1)} %get-tuple-element.25), channel_id=1, source_target_pairs={{8,0},{16,8},{24,16},{32,24},{40,32},{48,40},{56,48},{64,56},{72,6... | collective-permute-start | bytes 24584 | tf_op jit(solution)/shard_map/ppermute | solution.py:451
  52.9 0.0 collective-permute-done.1.above
  52.9 2.4 %collective-permute-done.2.below = f32[16,128]{1,0:T(8,128)S(1)} collective-permute-done((f32[16,128]{1,0:T(8,128)S(1)}, f32[16,128]{1,0:T(8,128)S(1)}, u32[]{:S(2)}, u32[]{:S(2)}) %collective-permute-start.2) | collective-permute-done | bytes 8224 | tf_op jit(solution)/shard_map/ppermute | solution.py:451
  55.3 5.4 %krylov.1 = (f32[48,128]{1,0:T(8,128)S(1)}, f32[48,128]{1,0:T(8,128)S(1)}, f32[48,128]{1,0:T(8,128)S(1)}, f32[128,16]{1,0:T(8,128)S(1)}) custom-call(f32[512,128]{1,0:T(8,128)S(1)} %bitcast.7, f32[3888,128]{1,0:T(8,128)S(1)} %get-tuple-element.18.factors, bf16[6,128,3072]{2,1,0:T(8,128)(2,1)S(1)} %get-tuple-element.19.hot_lane, ...), custom_call_target="tpu_custom_call" | custom-call | tf_op jit(solution)/shard_map/krylov/pallas_call | solution.py:452
  60.7 32.7 %all_to_all.17 = f32[128,1,16]{2,1,0:T(1,128)S(1)} all-to-all(f32[128,1,16]{2,1,0:T(1,128)S(1)} %bitcast.9), channel_id=1, replica_groups=mesh['patch'=128,'elem'=8] {'patch'}, dimensions={0} | all-to-all | bytes 16384 | tf_op jit(solution)/shard_map/all_to_all | solution.py:458
  93.3 1.1 %finish.1 = (f32[3,256]{1,0:T(4,128)}, f32[3,256]{1,0:T(4,128)}) custom-call(f32[128,16]{1,0:T(8,128)S(1)} %bitcast.8, f32[48,128]{1,0:T(8,128)S(1)} %get-tuple-element.21.first, f32[48,128]{1,0:T(8,128)S(1)} %get-tuple-element.27.second, f32[48,128]{1,0:T(8,128)S(1)} %get-tuple-element.28.third, f32[48,128]{1,0:T(8,128)S(1)} %get-tuple-element.29.last_image, ...), custom_call_target="tpu_custom_call" | custom-call | tf_op jit(solution)/shard_map/finish/pallas_call | solution.py:459
Async XLA Ops:
  0.6 18.3 %collective-permute-start = (f32[3,256]{1,0:T(4,128)}, f32[3,256]{1,0:T(4,128)S(1)}, u32[]{:S(2)}, u32[]{:S(2)}) collective-permute-start(f32[3,256]{1,0:T(4,128)} %pos.1), channel_id=1, source_target_pairs={{7,15},{8,0},{15,23},{16,8},{23,31},{24,16},{31,39},{32,24},{39,47... | collective-permute-start | bytes 9224 | tf_op jit(solution)/shard_map/ppermute | solution.py:418
  19.0 0.6 copy-start.1
  36.4 0.9 copy-start
  48.4 4.5 %collective-permute-start.1 = (f32[16,128]{1,0:T(8,128)S(1)}, f32[16,128]{1,0:T(8,128)S(1)}, u32[]{:S(2)}, u32[]{:S(2)}) collective-permute-start(f32[16,128]{1,0:T(8,128)S(1)} %get-tuple-element.24), channel_id=1, source_target_pairs={{0,8},{8,16},{16,24},{24,32},{32,40},{40,48},{48,56},{56,64},{64,7... | collective-permute-start | bytes 24584 | tf_op jit(solution)/shard_map/ppermute | solution.py:450
  50.3 5.0 %collective-permute-start.2 = (f32[16,128]{1,0:T(8,128)S(1)}, f32[16,128]{1,0:T(8,128)S(1)}, u32[]{:S(2)}, u32[]{:S(2)}) collective-permute-start(f32[16,128]{1,0:T(8,128)S(1)} %get-tuple-element.25), channel_id=1, source_target_pairs={{8,0},{16,8},{24,16},{32,24},{40,32},{48,40},{56,48},{64,56},{72,6... | collective-permute-start | bytes 24584 | tf_op jit(solution)/shard_map/ppermute | solution.py:451

commit v5 on v4

--- a/solution.py
+++ b/solution.py
@@ -410,7 +410,7 @@
 
 def per_device(positions, target, inertia, incidence, rest_inverse, counts, w_in, w_hid1, w_hid2, w_out):
     patches = lax.axis_size("patch")
-    params = pltpu.CompilerParams(vmem_limit_bytes=16 * 1024 * 1024)
+    params = pltpu.CompilerParams(vmem_limit_bytes=20 * 1024 * 1024)
     moves = []
     for p in range(patches - 1):
         left, right = p * GROUPS, (p + 1) * GROUPS
@@ -424,7 +424,7 @@
         rim_kernel, grid=(1,), out_shape=shape(GROUPS, PACKED, LANES),
         in_specs=[pl.BlockSpec(memory_space=pl.ANY)] + vmem(1) + [pl.BlockSpec(memory_space=pltpu.SMEM)],
         out_specs=pl.BlockSpec((GROUPS, PACKED - RIM, LANES), lambda i: (0, RIM // (PACKED - RIM), 0)),
-        input_output_aliases={0: 0}, name="rim",
+        input_output_aliases={0: 0}, compiler_params=params, name="rim",
     )(packed, rim, counts)
     whole = lax.all_to_all(packed, "elem", 0, 0, tiled=True).reshape(GROUPS * PACKED, LANES)
     wide = 3 * ROWS

time: 94.9 us -> 94.2 us (level)
    pallas_call x1, Pallas kernels: 1.3 us -> 0.01 us  [per_device(): pl.pallas_call(rim_kernel, grid=(1,), out_shape=shape(GROUPS, PACKED, LAN...]
where the time goes in v5:
time: 94.2 us; the launch traced here: 93.8 us
  blocking collectives  48 us (51%)
  starting transfers between devices  20.6 us (22%)
  Pallas kernels  19.7 us (21%)
  waiting for transfers between devices  2.37 us (3%)
  local copies, waits for them, and re-layouts  1.84 us (2%)
  between operations  1.32 us (1%)
    all_to_all x1, blocking collectives, per_device(): sums = lax.all_to_all(sums, 'patch', 0, 0, tiled=True)  33.4 us
    ppermute x1, starting transfers between devices, per_device(): rim = lax.ppermute(positions, ('patch', 'elem'), moves)  16.1 us
    all_to_all x1, blocking collectives, per_device(): lax.all_to_all(packed, 'elem', 0, 0, tiled=True)  14.7 us
    pallas_call x1, Pallas kernels, per_device(): pl.pallas_call(setup_kernel, out_shape=[shape(81 * TRI_ROWS, LANES), jax....  11.3 us
    pallas_call x1, Pallas kernels, per_device(): pl.pallas_call(krylov_kernel, out_shape=[shape(wide, LANES), shape(wide,...  5.74 us
    ppermute x1, starting transfers between devices, per_device(): lax.ppermute(down, 'patch', [(p + 1, p) for p in range(patches - 1)])  2.58 us
    ppermute x1, waiting for transfers between devices, per_device(): lax.ppermute(down, 'patch', [(p + 1, p) for p in range(patches - 1)])  2.37 us
    ppermute x1, starting transfers between devices, per_device(): above = lax.ppermute(up, 'patch', [(p, p + 1) for p in range(patches - 1)])  1.92 us
  transfers between devices with their start and end apart: 3, of which 1 were waited for; matrix products, arithmetic and copies ran while one was open for 0% of the time, Pallas kernels for 2%

profile of v5, /device:TPU:1, one launch (start us, length us, event | category | flops | bytes accessed | tf_op | source)
XLA Modules:
  0.0 93.8 jit_solution(15876390985651975485)
XLA Ops:
  0.6 16.1 %collective-permute-start = (f32[3,256]{1,0:T(4,128)}, f32[3,256]{1,0:T(4,128)S(1)}, u32[]{:S(2)}, u32[]{:S(2)}) collective-permute-start(f32[3,256]{1,0:T(4,128)} %pos.1), channel_id=1, source_target_pairs={{7,15},{8,0},{15,23},{16,8},{23,31},{24,16},{31,39},{32,24},{39,47... | collective-permute-start | bytes 9224 | tf_op jit(solution)/shard_map/ppermute | solution.py:418
  17.3 1.6 %pack.1 = (f32[8,64,128]{2,1,0:T(8,128)}, bf16[368,128]{1,0:T(8,128)(2,1)}) custom-call(f32[3,256]{1,0:T(4,128)} %pos.1, f32[3,256]{1,0:T(4,128)} %tgt.1, f32[1,256]{1,0:T(1,128)} %inertia.1, s32[3,768]{1,0:T(4,128)} %inc.1, f32[4,768]{1,0:T(4,128)} %rinv.1, bf16[6,128]{1,0:T(8,128)(2,1)} %bitcast.10, bf16[128,128]{1,0:T(8,128)(2,1)} %w_hid1.1, ...), custom_call_target="tpu_custom_call" | custom-call | tf_op jit(solution)/shard_map/pack/pallas_call | solution.py:419
  19.0 0.0 collective-permute-done.rim
  19.0 0.0 copy-start
  19.0 0.9 %copy-done = f32[8,64,128]{2,1,0:T(8,128)S(1)} copy-done((f32[8,64,128]{2,1,0:T(8,128)S(1)}, f32[8,64,128]{2,1,0:T(8,128)}, u32[]{:S(2)}) %copy-start) | copy-done | bytes 262168
  19.9 14.7 %all_to_all.16 = f32[8,64,128]{2,1,0:T(8,128)S(1)} all-to-all(f32[8,64,128]{2,1,0:T(8,128)S(1)} %rim.1), channel_id=1, replica_groups=mesh['patch'=128,'elem'=8] {'elem'}, dimensions={0} | all-to-all | bytes 524288 | tf_op jit(solution)/shard_map/all_to_all | solution.py:429
  34.6 0.0 copy-start.1
  34.6 0.9 copy-done.1
  35.5 11.3 %setup.1 = (f32[3888,128]{1,0:T(8,128)S(1)}, bf16[6,128,3072]{2,1,0:T(8,128)(2,1)S(1)}, bf16[6,16,3072]{2,1,0:T(8,128)(2,1)S(1)}, f32[48,128]{1,0:T(8,128)S(1)},...) custom-call(f32[512,128]{1,0:T(8,128)S(1)} %bitcast.6, ...), custom_call_target="tpu_custom_call" | custom-call | tf_op jit(solution)/shard_map/setup/pallas_call | solution.py:439
  46.7 1.9 %collective-permute-start.1 = (f32[16,128]{1,0:T(8,128)S(1)}, f32[16,128]{1,0:T(8,128)S(1)}, u32[]{:S(2)}, u32[]{:S(2)}) collective-permute-start(f32[16,128]{1,0:T(8,128)S(1)} %get-tuple-element.24), channel_id=1, source_target_pairs={{0,8},{8,16},{16,24},{24,32},{32,40},{40,48},{48,56},{56,64},{64,7... | collective-permute-start | bytes 24584 | tf_op jit(solution)/shard_map/ppermute | solution.py:450
  48.7 2.6 %collective-permute-start.2 = (f32[16,128]{1,0:T(8,128)S(1)}, f32[16,128]{1,0:T(8,128)S(1)}, u32[]{:S(2)}, u32[]{:S(2)}) collective-permute-start(f32[16,128]{1,0:T(8,128)S(1)} %get-tuple-element.25), channel_id=1, source_target_pairs={{8,0},{16,8},{24,16},{32,24},{40,32},{48,40},{56,48},{64,56},{72,6... | collective-permute-start | bytes 24584 | tf_op jit(solution)/shard_map/ppermute | solution.py:451
  51.3 0.0 collective-permute-done.1.above
  51.3 2.4 %collective-permute-done.2.below = f32[16,128]{1,0:T(8,128)S(1)} collective-permute-done((f32[16,128]{1,0:T(8,128)S(1)}, f32[16,128]{1,0:T(8,128)S(1)}, u32[]{:S(2)}, u32[]{:S(2)}) %collective-permute-start.2) | collective-permute-done | bytes 8224 | tf_op jit(solution)/shard_map/ppermute | solution.py:451
  53.6 5.7 %krylov.1 = (f32[48,128]{1,0:T(8,128)S(1)}, f32[48,128]{1,0:T(8,128)S(1)}, f32[48,128]{1,0:T(8,128)S(1)}, f32[128,16]{1,0:T(8,128)S(1)}) custom-call(f32[512,128]{1,0:T(8,128)S(1)} %bitcast.7, f32[3888,128]{1,0:T(8,128)S(1)} %get-tuple-element.18.factors, bf16[6,128,3072]{2,1,0:T(8,128)(2,1)S(1)} %get-tuple-element.19.hot_lane, ...), custom_call_target="tpu_custom_call" | custom-call | tf_op jit(solution)/shard_map/krylov/pallas_call | solution.py:452
  59.4 33.4 %all_to_all.17 = f32[128,1,16]{2,1,0:T(1,128)S(1)} all-to-all(f32[128,1,16]{2,1,0:T(1,128)S(1)} %bitcast.9), channel_id=1, replica_groups=mesh['patch'=128,'elem'=8] {'patch'}, dimensions={0} | all-to-all | bytes 16384 | tf_op jit(solution)/shard_map/all_to_all | solution.py:458
  92.8 1.1 %finish.1 = (f32[3,256]{1,0:T(4,128)}, f32[3,256]{1,0:T(4,128)}) custom-call(f32[128,16]{1,0:T(8,128)S(1)} %bitcast.8, f32[48,128]{1,0:T(8,128)S(1)} %get-tuple-element.21.first, f32[48,128]{1,0:T(8,128)S(1)} %get-tuple-element.27.second, f32[48,128]{1,0:T(8,128)S(1)} %get-tuple-element.28.third, f32[48,128]{1,0:T(8,128)S(1)} %get-tuple-element.29.last_image, ...), custom_call_target="tpu_custom_call" | custom-call | tf_op jit(solution)/shard_map/finish/pallas_call | solution.py:459
  (1 shorter events, 0.0 us)
Async XLA Ops:
  0.6 18.3 %collective-permute-start = (f32[3,256]{1,0:T(4,128)}, f32[3,256]{1,0:T(4,128)S(1)}, u32[]{:S(2)}, u32[]{:S(2)}) collective-permute-start(f32[3,256]{1,0:T(4,128)} %pos.1), channel_id=1, source_target_pairs={{7,15},{8,0},{15,23},{16,8},{23,31},{24,16},{31,39},{32,24},{39,47... | collective-permute-start | bytes 9224 | tf_op jit(solution)/shard_map/ppermute | solution.py:418
  19.0 1.0 %copy-start = (f32[8,64,128]{2,1,0:T(8,128)S(1)}, f32[8,64,128]{2,1,0:T(8,128)}, u32[]{:S(2)}) copy-start(f32[8,64,128]{2,1,0:T(8,128)} %get-tuple-element.16.packed) | copy-start | bytes 786436
  34.6 0.9 copy-start.1
  46.7 4.5 %collective-permute-start.1 = (f32[16,128]{1,0:T(8,128)S(1)}, f32[16,128]{1,0:T(8,128)S(1)}, u32[]{:S(2)}, u32[]{:S(2)}) collective-permute-start(f32[16,128]{1,0:T(8,128)S(1)} %get-tuple-element.24), channel_id=1, source_target_pairs={{0,8},{8,16},{16,24},{24,32},{32,40},{40,48},{48,56},{56,64},{64,7... | collective-permute-start | bytes 24584 | tf_op jit(solution)/shard_map/ppermute | solution.py:450
  48.7 5.0 %collective-permute-start.2 = (f32[16,128]{1,0:T(8,128)S(1)}, f32[16,128]{1,0:T(8,128)S(1)}, u32[]{:S(2)}, u32[]{:S(2)}) collective-permute-start(f32[16,128]{1,0:T(8,128)S(1)} %get-tuple-element.25), channel_id=1, source_target_pairs={{8,0},{16,8},{24,16},{32,24},{40,32},{48,40},{56,48},{64,56},{72,6... | collective-permute-start | bytes 24584 | tf_op jit(solution)/shard_map/ppermute | solution.py:451

commit v6 on v5

--- a/solution.py
+++ b/solution.py
@@ -55,8 +55,8 @@
         out[e] = block
 
 
-def rim_kernel(packed, rim, counts, out):
-    del packed
+def rim_kernel(packed, rim, counts, weights, out, weights_out):
+    del packed, weights, weights_out
     first = lax.axis_index("elem") == 0
     ends = jnp.where(first, rim[:, :LANES], rim[:, LANES:])
     count = jnp.full((1, LANES), counts[0], jnp.int32).astype(F32)
@@ -420,12 +420,15 @@
         pack_kernel, out_shape=[shape(GROUPS, PACKED, LANES), jax.ShapeDtypeStruct((WEIGHTS, LANES), BF16)],
         in_specs=vmem(9), out_specs=vmem(2), name="pack",
     )(positions, target, inertia, incidence, rest_inverse, w_in.T, w_hid1, w_hid2, w_out)
-    packed = pl.pallas_call(
-        rim_kernel, grid=(1,), out_shape=shape(GROUPS, PACKED, LANES),
-        in_specs=[pl.BlockSpec(memory_space=pl.ANY)] + vmem(1) + [pl.BlockSpec(memory_space=pltpu.SMEM)],
-        out_specs=pl.BlockSpec((GROUPS, PACKED - RIM, LANES), lambda i: (0, RIM // (PACKED - RIM), 0)),
-        input_output_aliases={0: 0}, compiler_params=params, name="rim",
-    )(packed, rim, counts)
+    packed, weights = pl.pallas_call(
+        rim_kernel, grid=(1,),
+        out_shape=[shape(GROUPS, PACKED, LANES), jax.ShapeDtypeStruct(weights.shape, weights.dtype)],
+        in_specs=[pl.BlockSpec(memory_space=pl.ANY)] + vmem(1) + [pl.BlockSpec(memory_space=pltpu.SMEM)]
+        + [pl.BlockSpec(memory_space=pl.ANY)],
+        out_specs=[pl.BlockSpec((GROUPS, PACKED - RIM, LANES), lambda i: (0, RIM // (PACKED - RIM), 0)),
+                   pl.BlockSpec(memory_space=pl.ANY)],
+        input_output_aliases={0: 0, 3: 1}, compiler_params=params, name="rim",
+    )(packed, rim, counts, weights)
     whole = lax.all_to_all(packed, "elem", 0, 0, tiled=True).reshape(GROUPS * PACKED, LANES)
     wide = 3 * ROWS
     width = GROUPS * LANES

time: 94.2 us -> 95.2 us (1.011)
    unnamed x4 -> x8, local copies, waits for them, and re-layouts: 1.84 us -> 2.73 us
where the time goes in v6:
time: 95.2 us; the launch traced here: 94.7 us
  blocking collectives  48 us (50%)
  starting transfers between devices  20.6 us (22%)
  Pallas kernels  19.7 us (21%)
  local copies, waits for them, and re-layouts  2.73 us (3%)
  waiting for transfers between devices  2.37 us (2%)
  between operations  1.33 us (1%)
    all_to_all x1, blocking collectives, per_device(): sums = lax.all_to_all(sums, 'patch', 0, 0, tiled=True)  33.4 us
    ppermute x1, starting transfers between devices, per_device(): rim = lax.ppermute(positions, ('patch', 'elem'), moves)  16.1 us
    all_to_all x1, blocking collectives, per_device(): lax.all_to_all(packed, 'elem', 0, 0, tiled=True)  14.7 us
    pallas_call x1, Pallas kernels, per_device(): pl.pallas_call(setup_kernel, out_shape=[shape(81 * TRI_ROWS, LANES), jax....  11.3 us
    pallas_call x1, Pallas kernels, per_device(): pl.pallas_call(krylov_kernel, out_shape=[shape(wide, LANES), shape(wide,...  5.74 us
    unnamed x8, local copies, waits for them, and re-layouts  2.73 us
    ppermute x1, starting transfers between devices, per_device(): lax.ppermute(down, 'patch', [(p + 1, p) for p in range(patches - 1)])  2.58 us
    ppermute x1, waiting for transfers between devices, per_device(): lax.ppermute(down, 'patch', [(p + 1, p) for p in range(patches - 1)])  2.37 us
  transfers between devices with their start and end apart: 3, of which 1 were waited for; matrix products, arithmetic and copies ran while one was open for 0% of the time, Pallas kernels for 2%

profile of v6, /device:TPU:1, one launch (start us, length us, event | category | flops | bytes accessed | tf_op | source)
XLA Modules:
  0.0 94.7 jit_solution(6347217363699772739)
XLA Ops:
  0.6 16.1 %collective-permute-start = (f32[3,256]{1,0:T(4,128)}, f32[3,256]{1,0:T(4,128)S(1)}, u32[]{:S(2)}, u32[]{:S(2)}) collective-permute-start(f32[3,256]{1,0:T(4,128)} %pos.1), channel_id=1, source_target_pairs={{7,15},{8,0},{15,23},{16,8},{23,31},{24,16},{31,39},{32,24},{39,47... | collective-permute-start | bytes 9224 | tf_op jit(solution)/shard_map/ppermute | solution.py:418
  17.3 1.6 %pack.1 = (f32[8,64,128]{2,1,0:T(8,128)}, bf16[368,128]{1,0:T(8,128)(2,1)}) custom-call(f32[3,256]{1,0:T(4,128)} %pos.1, f32[3,256]{1,0:T(4,128)} %tgt.1, f32[1,256]{1,0:T(1,128)} %inertia.1, s32[3,768]{1,0:T(4,128)} %inc.1, f32[4,768]{1,0:T(4,128)} %rinv.1, bf16[6,128]{1,0:T(8,128)(2,1)} %bitcast.10, bf16[128,128]{1,0:T(8,128)(2,1)} %w_hid1.1, ...), custom_call_target="tpu_custom_call" | custom-call | tf_op jit(solution)/shard_map/pack/pallas_call | solution.py:419
  19.0 0.0 collective-permute-done.rim
  19.0 0.0 copy-start
  19.0 0.9 copy-done
  19.9 0.0 copy-start.1
  19.9 0.9 copy-done.1
  20.8 0.0 copy-start.2
  20.8 14.7 %all_to_all.16 = f32[8,64,128]{2,1,0:T(8,128)S(1)} all-to-all(f32[8,64,128]{2,1,0:T(8,128)S(1)} %get-tuple-element.20), channel_id=1, replica_groups=mesh['patch'=128,'elem'=8] {'elem'}, dimensions={0} | all-to-all | bytes 524288 | tf_op jit(solution)/shard_map/all_to_all | solution.py:432
  35.5 0.0 copy-done.2
  35.5 0.0 copy-start.3
  35.5 0.9 copy-done.3
  36.4 11.3 %setup.1 = (f32[3888,128]{1,0:T(8,128)S(1)}, bf16[6,128,3072]{2,1,0:T(8,128)(2,1)S(1)}, bf16[6,16,3072]{2,1,0:T(8,128)(2,1)S(1)}, f32[48,128]{1,0:T(8,128)S(1)},...) custom-call(f32[512,128]{1,0:T(8,128)S(1)} %bitcast.6, ...), custom_call_target="tpu_custom_call" | custom-call | tf_op jit(solution)/shard_map/setup/pallas_call | solution.py:442
  47.7 1.9 %collective-permute-start.1 = (f32[16,128]{1,0:T(8,128)S(1)}, f32[16,128]{1,0:T(8,128)S(1)}, u32[]{:S(2)}, u32[]{:S(2)}) collective-permute-start(f32[16,128]{1,0:T(8,128)S(1)} %get-tuple-element.28), channel_id=1, source_target_pairs={{0,8},{8,16},{16,24},{24,32},{32,40},{40,48},{48,56},{56,64},{64,7... | collective-permute-start | bytes 24584 | tf_op jit(solution)/shard_map/ppermute | solution.py:453
  49.6 2.6 %collective-permute-start.2 = (f32[16,128]{1,0:T(8,128)S(1)}, f32[16,128]{1,0:T(8,128)S(1)}, u32[]{:S(2)}, u32[]{:S(2)}) collective-permute-start(f32[16,128]{1,0:T(8,128)S(1)} %get-tuple-element.29), channel_id=1, source_target_pairs={{8,0},{16,8},{24,16},{32,24},{40,32},{48,40},{56,48},{64,56},{72,6... | collective-permute-start | bytes 24584 | tf_op jit(solution)/shard_map/ppermute | solution.py:454
  52.2 0.0 collective-permute-done.1.above
  52.2 2.4 %collective-permute-done.2.below = f32[16,128]{1,0:T(8,128)S(1)} collective-permute-done((f32[16,128]{1,0:T(8,128)S(1)}, f32[16,128]{1,0:T(8,128)S(1)}, u32[]{:S(2)}, u32[]{:S(2)}) %collective-permute-start.2) | collective-permute-done | bytes 8224 | tf_op jit(solution)/shard_map/ppermute | solution.py:454
  54.6 5.7 %krylov.1 = (f32[48,128]{1,0:T(8,128)S(1)}, f32[48,128]{1,0:T(8,128)S(1)}, f32[48,128]{1,0:T(8,128)S(1)}, f32[128,16]{1,0:T(8,128)S(1)}) custom-call(f32[512,128]{1,0:T(8,128)S(1)} %bitcast.7, f32[3888,128]{1,0:T(8,128)S(1)} %get-tuple-element.22.factors, bf16[6,128,3072]{2,1,0:T(8,128)(2,1)S(1)} %get-tuple-element.23.hot_lane, ...), custom_call_target="tpu_custom_call" | custom-call | tf_op jit(solution)/shard_map/krylov/pallas_call | solution.py:455
  60.3 33.4 %all_to_all.17 = f32[128,1,16]{2,1,0:T(1,128)S(1)} all-to-all(f32[128,1,16]{2,1,0:T(1,128)S(1)} %bitcast.9), channel_id=1, replica_groups=mesh['patch'=128,'elem'=8] {'patch'}, dimensions={0} | all-to-all | bytes 16384 | tf_op jit(solution)/shard_map/all_to_all | solution.py:461
  93.7 1.1 %finish.1 = (f32[3,256]{1,0:T(4,128)}, f32[3,256]{1,0:T(4,128)}) custom-call(f32[128,16]{1,0:T(8,128)S(1)} %bitcast.8, f32[48,128]{1,0:T(8,128)S(1)} %get-tuple-element.25.first, f32[48,128]{1,0:T(8,128)S(1)} %get-tuple-element.31.second, f32[48,128]{1,0:T(8,128)S(1)} %get-tuple-element.32.third, f32[48,128]{1,0:T(8,128)S(1)} %get-tuple-element.33.last_image, ...), custom_call_target="tpu_custom_call" | custom-call | tf_op jit(solution)/shard_map/finish/pallas_call | solution.py:462
  (1 shorter events, 0.0 us)
Async XLA Ops:
  0.6 18.4 %collective-permute-start = (f32[3,256]{1,0:T(4,128)}, f32[3,256]{1,0:T(4,128)S(1)}, u32[]{:S(2)}, u32[]{:S(2)}) collective-permute-start(f32[3,256]{1,0:T(4,128)} %pos.1), channel_id=1, source_target_pairs={{7,15},{8,0},{15,23},{16,8},{23,31},{24,16},{31,39},{32,24},{39,47... | collective-permute-start | bytes 9224 | tf_op jit(solution)/shard_map/ppermute | solution.py:418
  19.0 1.0 %copy-start = (f32[8,64,128]{2,1,0:T(8,128)S(1)}, f32[8,64,128]{2,1,0:T(8,128)}, u32[]{:S(2)}) copy-start(f32[8,64,128]{2,1,0:T(8,128)} %get-tuple-element.18.packed) | copy-start | bytes 786436
  19.9 0.9 copy-start.1
  20.8 14.7 %copy-start.2 = (bf16[368,128]{1,0:T(8,128)(2,1)}, bf16[368,128]{1,0:T(8,128)(2,1)S(1)}, u32[]{:S(2)}) copy-start(bf16[368,128]{1,0:T(8,128)(2,1)S(1)} %get-tuple-element.21.weights) | copy-start | bytes 282628
  35.5 0.9 copy-start.3
  47.7 4.5 %collective-permute-start.1 = (f32[16,128]{1,0:T(8,128)S(1)}, f32[16,128]{1,0:T(8,128)S(1)}, u32[]{:S(2)}, u32[]{:S(2)}) collective-permute-start(f32[16,128]{1,0:T(8,128)S(1)} %get-tuple-element.28), channel_id=1, source_target_pairs={{0,8},{8,16},{16,24},{24,32},{32,40},{40,48},{48,56},{56,64},{64,7... | collective-permute-start | bytes 24584 | tf_op jit(solution)/shard_map/ppermute | solution.py:453
  49.6 5.0 %collective-permute-start.2 = (f32[16,128]{1,0:T(8,128)S(1)}, f32[16,128]{1,0:T(8,128)S(1)}, u32[]{:S(2)}, u32[]{:S(2)}) collective-permute-start(f32[16,128]{1,0:T(8,128)S(1)} %get-tuple-element.29), channel_id=1, source_target_pairs={{8,0},{16,8},{24,16},{32,24},{40,32},{48,40},{56,48},{64,56},{72,6... | collective-permute-start | bytes 24584 | tf_op jit(solution)/shard_map/ppermute | solution.py:454
